TPU v7x, 256 devices: a whole 4x4x8 slice. The times are simulated.
256 devices in a mesh: dp: 64 (over x, z, core), fsdp: 4 (over y).
Axes of the slice: x: 4, y: 4, z: 8, core: 2. Of those that a mesh axis runs over, the one named last changes fastest.
Arguments:
- item_states: bfloat16 [256, 256, 4096], P('dp', None, 'fsdp'), may hold values from -6 to 6
- item_scores: float32 [256, 16, 256], P('dp'), may hold values from -8 to 8
- item_lengths: int32 [256], P('dp'), may hold values from 1 to 256, 32768 in all
- item_gain: float32 [4096], P('fsdp'), may hold values from 0.25 to 1.75
- value_weight: bfloat16 [4096, 2048], P('fsdp'), may hold values from -0.09375 to 0.09375
- user_items: int32 [64, 1024], P('dp', 'fsdp'), may hold values from 0 to 255
- negatives: int32 [64, 256], P('dp'), may hold values from 0 to 255
- position_embed: bfloat16 [1024, 2048], P('fsdp'), may hold values from -3 to 3
- user_gain: float32 [2048], replicated, may hold values from 0.25 to 1.75
- user_weight: bfloat16 [2048, 2048], P('fsdp'), may hold values from -0.125 to 0.125
Outputs:
- item_grads: float32 [256, 2048], P('dp')
- weight_grad: bfloat16 [2048, 2048], P('fsdp')
Inputs may be any that keep to these rules, and one draw needn't show every extreme that they name: `user_items`: item ids of the catalogue. `negatives`: item ids of the catalogue. `item_lengths`: one or more tokens of each text are used.
All inputs are finite; a program needn't handle non-finite values. No bound on the sum of `item_lengths` on one device may be relied on, other than what follows from the above.
Results may differ from a plain program's by a relative error of at most 0.022.
Values may be sent and summed in bfloat16 or wider, within the bound.
A program may use at most 128 MiB of HBM per device.

v0:
```python
import jax
import jax.numpy as jnp
from jax import lax
from jax.sharding import PartitionSpec as P

D = 4096
ULEN = 1024


def from_behind(block, axis, distance):
    devices = range(lax.axis_size(axis))
    route = [(i - distance, i) for i in devices if i - distance in devices]
    return lax.ppermute(block, axis, route)


def unit_rows(vectors):
    length = jnp.sqrt(jnp.sum(vectors * vectors, axis=1, keepdims=True) + 1e-06)
    return (vectors / length, length)


def contract_first(left, right, precision=None):
    return lax.dot_general(
        left,
        right,
        (((0,), (0,)), ((), ())),
        precision=precision,
        preferred_element_type=jnp.float32,
    )


def local(
    item_states,
    item_scores,
    item_lengths,
    item_gain,
    value_weight,
    user_items,
    negatives,
    position_embed,
    user_gain,
    user_weight,
):
    owners = lax.axis_size("dp")
    local_items, text_len, feat_part = item_states.shape
    width = value_weight.shape[1]
    heads = item_scores.shape[1]
    highest = lax.Precision.HIGHEST
    full_weight = lax.all_gather(user_weight, "fsdp", axis=0, tiled=True)
    states_f = item_states.astype(jnp.float32)
    squares = jnp.sum(states_f * states_f, axis=2)
    scaled = (states_f * item_gain).astype(jnp.bfloat16)
    values = jnp.dot(
        scaled.reshape(local_items * text_len, feat_part),
        value_weight,
        preferred_element_type=jnp.float32,
    )
    whole_squares = lax.psum(squares, "fsdp")
    inv_rms = lax.rsqrt(whole_squares / D + 1e-05)
    position = jnp.arange(text_len)
    weights = jnp.where(
        position[None, None, :] < item_lengths[:, None, None], jnp.exp(item_scores), 0.0
    )
    values = values.reshape(local_items, text_len, heads, width // heads)
    numerator = jnp.einsum("iht,ithc->ihc", weights * inv_rms[:, None, :], values)
    numerator = lax.psum(numerator, "fsdp")
    totals = jnp.sum(weights, axis=2)
    item_embed = (numerator / totals[:, :, None]).reshape(local_items, width).astype(jnp.bfloat16)
    fsdp_index = lax.axis_index("fsdp")
    catalog_rows = lax.all_gather(item_embed, "dp", axis=0, tiled=True)
    item_ids = user_items[0]
    neg_ids = negatives[0]
    count_rows = item_ids.shape[0]
    user_rows = jnp.take(catalog_rows, item_ids, axis=0)
    next_first = from_behind(user_rows[:1], "fsdp", -1)
    rows_f = user_rows.astype(jnp.float32)
    input_f = rows_f + position_embed.astype(jnp.float32)
    inv_user = lax.rsqrt(jnp.mean(input_f * input_f, axis=1, keepdims=True) + 1e-05)
    user_normed = (input_f * inv_user * user_gain).astype(jnp.bfloat16)
    output = input_f + jnp.dot(user_normed, full_weight, preferred_element_type=jnp.float32)
    target = jnp.concatenate([rows_f[1:], next_first.astype(jnp.float32)], axis=0)
    neg_rows = jnp.take(catalog_rows, neg_ids, axis=0).astype(jnp.float32)
    global_rows = fsdp_index * count_rows + jnp.arange(count_rows)
    valid_rows = (global_rows < ULEN - 1).astype(jnp.float32)
    out_unit, out_len = unit_rows(output)
    tgt_unit, tgt_len = unit_rows(target)
    neg_unit, neg_len = unit_rows(neg_rows)
    pos_logit = 20.0 * jnp.sum(out_unit * tgt_unit, axis=1)
    neg_logit = 20.0 * lax.dot_general(
        out_unit,
        neg_unit,
        (((1,), (1,)), ((), ())),
        precision=highest,
        preferred_element_type=jnp.float32,
    )
    log_total = jnp.log(jnp.exp(pos_logit) + jnp.sum(jnp.exp(neg_logit), axis=1))
    scale_loss = 1.0 / (owners * (ULEN - 1))
    pos_grad = scale_loss * valid_rows * (jnp.exp(pos_logit - log_total) - 1.0)
    neg_grad = scale_loss * valid_rows[:, None] * jnp.exp(neg_logit - log_total[:, None])
    out_unit_grad = 20.0 * (
        pos_grad[:, None] * tgt_unit + jnp.dot(neg_grad, neg_unit, precision=highest)
    )
    tgt_unit_grad = 20.0 * pos_grad[:, None] * out_unit
    neg_unit_grad = 20.0 * contract_first(neg_grad, out_unit, highest)
    grad_out = (
        out_unit_grad - out_unit * jnp.sum(out_unit * out_unit_grad, axis=1, keepdims=True)
    ) / out_len
    tgt_grad = (
        tgt_unit_grad - tgt_unit * jnp.sum(tgt_unit * tgt_unit_grad, axis=1, keepdims=True)
    ) / tgt_len
    neg_row_grad = (
        neg_unit_grad - neg_unit * jnp.sum(neg_unit * neg_unit_grad, axis=1, keepdims=True)
    ) / neg_len
    grad_cast = grad_out.astype(jnp.bfloat16)
    weight_rows = lax.psum_scatter(
        contract_first(user_normed, grad_cast), "fsdp", scatter_dimension=0, tiled=True
    )
    weight_grad = lax.psum(weight_rows, "dp").astype(jnp.bfloat16)
    normed_grad = lax.dot_general(
        grad_cast, full_weight, (((1,), (1,)), ((), ())), preferred_element_type=jnp.float32
    )
    gained = user_gain * normed_grad
    grad_rows = (
        grad_out
        + inv_user * gained
        - input_f * inv_user**3 * jnp.mean(gained * input_f, axis=1, keepdims=True)
    )
    prev_last = from_behind(tgt_grad[-1:], "fsdp", 1)
    grad_rows = grad_rows + jnp.concatenate([prev_last, tgt_grad[:-1]], axis=0)
    row_cast = grad_rows.astype(jnp.bfloat16)
    item_count = catalog_rows.shape[0]
    catalog = jnp.arange(item_count)
    pos_onehot = (item_ids[:, None] == catalog[None, :]).astype(jnp.bfloat16)
    neg_onehot = (neg_ids[:, None] == catalog[None, :]).astype(jnp.float32)
    grad_term = contract_first(pos_onehot, row_cast) + contract_first(
        neg_onehot, neg_row_grad, highest
    )
    owned_part = lax.psum_scatter(grad_term, "dp", scatter_dimension=0, tiled=True)
    item_grads = lax.psum(owned_part, "fsdp")
    return (item_grads, weight_grad)


def solution(mesh):
    return jax.shard_map(
        local,
        mesh=mesh,
        in_specs=(
            P("dp", None, "fsdp"),
            P("dp", None, None),
            P("dp"),
            P("fsdp"),
            P("fsdp", None),
            P("dp", "fsdp"),
            P("dp", None),
            P("fsdp", None),
            P(),
            P("fsdp", None),
        ),
        out_specs=(P("dp", None), P("fsdp", None)),
        check_vma=False,
    )
```

profile of v0, /device:TPU:1, one launch (start us, length us, event | category | flops | bytes accessed | tf_op | source)
XLA Modules:
  0.0 883.8 jit_solution(4223398100521898589)
XLA Ops:
  7.2 0.0 all-gather.6.cloned.1.call-start
  7.2 0.7 iota_compare_fusion.4
  7.9 2.1 fusion
  10.0 9.6 %psum.28 = f32[4,256]{1,0:T(4,128)S(1)} all-reduce(f32[4,256]{1,0:T(4,128)S(1)} %fusion), channel_id=1, replica_groups=mesh['dp'=64,'fsdp'=4] {'fsdp'}, use_global_device_ids=true, to_apply=%region_1.0 | all-reduce | flops 1024 | bytes 8192 | tf_op jit(solution)/shard_map/psum | solution.py:57
  19.6 0.0 copy-done.8
  19.6 0.1 fusion.40
  19.7 0.0 copy-start.7
  19.7 0.0 copy-start.12
  19.8 5.7 copy.18
  25.4 7.2 fusion.5
  32.6 0.0 copy-start.11
  32.7 11.1 %psum.29 = f32[4,16,128]{2,1,0:T(8,128)S(1)} all-reduce(f32[4,16,128]{2,1,0:T(8,128)S(1)} %bitcast.25), channel_id=1, replica_groups=mesh['dp'=64,'fsdp'=4] {'fsdp'}, use_global_device_ids=true, to_apply=%region_2.3 | all-reduce | flops 8192 | bytes 65536 | tf_op jit(solution)/shard_map/psum | solution.py:65
  43.7 0.1 divide_convert_fusion
  43.8 0.6 reshape.133
  44.4 0.0 all-gather.6.cloned.1.call-update
  44.5 0.0 all-gather.4.cloned.1.call-start
  44.5 0.7 all-gather.4.cloned.1.call-update
  45.2 0.0 all-reduce.4.cloned.1.call-start
  45.3 0.0 copy-done.10
  45.3 0.0 copy-done.11
  45.4 83.2 %all-gather.6.cloned.1.call-done = bf16[64,4,2048]{2,1,0:T(4,128)(2,1)} async-done(((bf16[1,4,2048]{2,1,0:T(4,128)(2,1)}), bf16[64,4,2048]{2,1,0:T(4,128)(2,1)}) %all-gather.6.cloned.1.call-update) | async-done | bytes 1048592 | tf_op jit(solution)/shard_map/all_gather | solution.py:69
  128.6 1.3 reshape.134
  129.9 1.4 gather_fusion.1
  131.3 0.0 copy-start.4
  131.3 0.0 copy-start.2
  131.3 2.4 gather_fusion
  133.7 1.8 multiply_reduce_fusion.7
  135.6 1.5 collective-permute-start
  137.0 0.0 copy-done.4
  137.0 0.4 fusion.7
  137.5 0.3 slice.20
  137.8 0.0 copy-start.9
  137.8 2.1 collective-permute-done
  140.0 0.2 multiply_reduce_fusion.5
  140.2 73.3 %all-gather.4.cloned.1.call-done = bf16[2048,2048]{1,0:T(8,128)(2,1)} async-done(((bf16[512,2048]{1,0:T(8,128)(2,1)}), bf16[2048,2048]{1,0:T(8,128)(2,1)}) %all-gather.4.cloned.1.call-update) | async-done | bytes 8388624 | tf_op jit(solution)/shard_map/all_gather | solution.py:48
  213.5 6.5 multiply_reduce_fusion.6
  220.0 0.0 copy-start.5
  220.0 0.5 multiply_reduce_fusion.4
  220.5 1.5 copy-done.5
  222.0 2.2 exponential_reduce_fusion
  224.2 2.5 multiply_reduce_fusion
  226.7 3.0 multiply_reduce_fusion.3
  229.7 0.0 slice-start
  229.7 0.5 subtract_divide_fusion
  230.2 3.6 collective-permute-start.1
  233.8 0.0 copy-start.3
  233.8 0.0 slice-start.1
  233.8 1.8 fusion.12
  235.7 0.6 slice-done.1
  236.3 3.9 multiply_reduce_fusion.2
  240.3 0.0 collective-permute-done.1
  240.3 4.6 convolution_add_fusion
  244.9 0.0 all-reduce.4.cloned.1.call-update
  245.0 0.0 reduce-scatter.2.cloned.1.call-start
  245.0 1.5 copy-done.1
  246.5 10.3 %fusion.19 = f32[2048,2048]{1,0:T(8,128)} fusion(f32[2048]{0:T(1024)S(1)} %copy-done.9, f32[256]{0:T(256)S(1)} %get-tuple-element.11, bf16[256,2048]{1,0:T(8,128)(2,1)} %param.19, bf16[256,2048]{1,0:T(8,128)(2,1)S(1)} %get-tuple-element.8, f32[256,2048]{1,0:T(8,128)} %copy-done.6, f32[256]{0:T(256)S(1)} %get-tuple-element.3, f32[256]{0:T(256)S(1)} %add_sqrt_fusion.2, ...), kind=kOutput, calls=%fused_computation.39 | convolution fusion | flops 2153250816 | bytes 23079936 | tf_op jit(solution)/shard_map/dot_general | solution.py:22
  256.8 0.0 reduce-scatter.2.cloned.1.call-update
  256.9 0.6 copy-done.13
  257.5 0.6 dynamic-slice
  258.7 174.6 %all-reduce.4.cloned.1.call-done = f32[256,2048]{1,0:T(8,128)} async-done(((f32[256,2048]{1,0:T(8,128)}), f32[256,2048]{1,0:T(8,128)}) %all-reduce.4.cloned.1.call-update) | async-done | bytes 2097168
  433.4 0.8 constant_dynamic-slice_fusion
  434.2 13.9 %psum.30 = f32[4,2048]{1,0:T(4,128)} all-reduce(f32[4,2048]{1,0:T(4,128)S(1)} %constant_dynamic-slice_fusion), channel_id=1, replica_groups=mesh['dp'=64,'fsdp'=4] {'fsdp'}, use_global_device_ids=true, to_apply=%region_15.17 | all-reduce | flops 8192 | bytes 65536 | tf_op jit(solution)/shard_map/psum | solution.py:138
  448.1 138.7 %reduce-scatter.2.cloned.1.call-done = f32[512,2048]{1,0:T(8,128)} async-done(((f32[2048,2048]{1,0:T(8,128)}), f32[512,2048]{1,0:T(8,128)}) %reduce-scatter.2.cloned.1.call-update) | async-done | bytes 4194320 | tf_op jit(solution)/shard_map/reduce_scatter | solution.py:114
  586.8 290.5 %all-reduce.5 = bf16[512,2048]{1,0:T(8,128)(2,1)} all-reduce(f32[512,2048]{1,0:T(8,128)} %reduce-scatter.2.cloned.1.call-done), channel_id=1, replica_groups=mesh['dp'=64,'fsdp'=4] {'dp'}, use_global_device_ids=true, to_apply=%region_17.19 | all-reduce | flops 1048576 | bytes 6291456 | tf_op jit(solution)/shard_map/psum | solution.py:117
  (33 shorter events, 0.2 us)
Async XLA Ops:
  7.2 12.4 %copy-start.8 = (f32[4,16,256]{2,1,0:T(8,128)S(1)}, f32[4,16,256]{2,1,0:T(8,128)}, u32[]{:S(2)}) copy-start(f32[4,16,256]{2,1,0:T(8,128)} %param.13) | copy-start | bytes 196612
  7.2 121.4 %all-gather.6.cloned.1.call-start = ((), (), s32[]{:S(2)}) async-start(), calls=%async_computation.3 | async-start | bytes 1064960 | tf_op jit(solution)/shard_map/all_gather | solution.py:69
  19.7 5.7 copy-start.7
  19.7 5.7 copy-start.12
  32.6 12.6 %copy-start.10 = (s32[1,256]{1,0:T(1,128)S(1)}, s32[1,256]{1,0:T(1,128)}, u32[]{:S(2)}) copy-start(s32[1,256]{1,0:T(1,128)} %param.18) | copy-start | bytes 3076
  32.6 12.7 %copy-start.11 = (s32[1,256]{1,0:T(1,128)S(1)}, s32[1,256]{1,0:T(1,128)}, u32[]{:S(2)}) copy-start(s32[1,256]{1,0:T(1,128)} %param.17) | copy-start | bytes 3076
  44.5 169.0 %all-gather.4.cloned.1.call-start = ((), (), s32[]{:S(2)}) async-start(), calls=%async_computation.1 | async-start | bytes 10485760 | tf_op jit(solution)/shard_map/all_gather | solution.py:48
  45.2 388.1 %all-reduce.4.cloned.1.call-start = ((), (), s32[]{:S(2)}) async-start(), calls=%async_computation.4 | async-start | bytes 4194304
  131.3 5.8 copy-start.4
  131.3 2.4 copy-start.2
  135.6 4.4 collective-permute-start
  137.8 75.7 %copy-start.9 = (f32[2048]{0:T(1024)S(1)}, f32[2048]{0:T(1024)}, u32[]{:S(2)}) copy-start(f32[2048]{0:T(1024)} %param.20) | copy-start | bytes 24580
  219.9 20.3 %copy-start = (f32[256,2048]{1,0:T(8,128)}, f32[256,2048]{1,0:T(8,128)S(1)}, u32[]{:S(2)}) copy-start(f32[256,2048]{1,0:T(8,128)S(1)} %get-tuple-element.13) | copy-start | bytes 6291460
  220.0 2.0 copy-start.5
  229.6 10.6 %copy-start.6 = (f32[256,2048]{1,0:T(8,128)}, f32[256,2048]{1,0:T(8,128)S(1)}, u32[]{:S(2)}) copy-start(f32[256,2048]{1,0:T(8,128)S(1)} %get-tuple-element.18) | copy-start | bytes 6291460
  229.7 6.0 slice-start
  230.2 10.1 %collective-permute-start.1 = (f32[1,2048]{1,0:T(1,128)S(1)}, f32[1,2048]{1,0:T(1,128)S(1)}, u32[]{:S(2)}, u32[]{:S(2)}) collective-permute-start(f32[1,2048]{1,0:T(1,128)S(1)} %slice.22), channel_id=1, source_target_pairs={{0,1},{1,2},{2,3},{4,5},{5,6},{6,7},{8,9},{9,10},{10,11},{12,13},{... | collective-permute-start | bytes 24584 | tf_op jit(solution)/shard_map/ppermute | solution.py:13
  233.8 1.9 copy-start.3
  233.8 2.5 slice-start.1
  244.9 1.6 copy-start.1
  245.0 341.8 %reduce-scatter.2.cloned.1.call-start = ((), (), s32[]{:S(2)}) async-start(), calls=%async_computation.2 | async-start | bytes 20971520 | tf_op jit(solution)/shard_map/reduce_scatter | solution.py:114
  256.8 0.7 copy-start.13
Sparse Core Ops, SparseCore 0:
  44.6 83.9 all-gather.5
  130.4 83.0 all-gather.3
  245.1 188.2 all-reduce.3
  435.8 150.9 reduce-scatter.1
where the time goes:
time: 888 us; the launch traced here: 884 us
  waiting for transfers between devices  473 us (53%)
  blocking collectives  325 us (37%)
  matrix products  42 us (5%)
  local copies, waits for them, and re-layouts  17.5 us (2%)
  between operations  14.8 us (2%)
    psum x1, blocking collectives, local(): weight_grad = lax.psum(weight_rows, 'dp').astype(jnp.bfloat16)  290 us
    unnamed x5, waiting for transfers between devices  175 us
    reduce_scatter x1, waiting for transfers between devices, local(): lax.psum_scatter(contract_first(user_normed, grad_cast), 'fsdp', scatter_...  139 us
    all_gather x1, waiting for transfers between devices, local(): catalog_rows = lax.all_gather(item_embed, 'dp', axis=0, tiled=True)  83.2 us
    all_gather x1, waiting for transfers between devices, local(): full_weight = lax.all_gather(user_weight, 'fsdp', axis=0, tiled=True)  73.3 us
    dot_general x4, matrix products, contract_first(): lax.dot_general(left, right, (((0,), (0,)), ((), ())), precision=precisio...  19.3 us
  transfers between devices with their start and end apart: 6, of which 5 were waited for; matrix products, arithmetic and copies ran while one was open for 3% of the time, Pallas kernels for 0%

commit v1 on v0

v1 whole, which is shorter than its diff:
```python
import jax
import jax.numpy as jnp
from jax import lax
from jax.experimental import pallas as pl
from jax.experimental.pallas import tpu as pltpu
from jax.sharding import PartitionSpec as P

MESH = pl.DeviceIdType.MESH
F32, BF16 = jnp.float32, jnp.bfloat16
NX, NY, NZ = 4, 4, 8
D, HV, ULEN, USERS = 4096, 2048, 1024, 64
VM = pl.BlockSpec(memory_space=pltpu.VMEM)
ANY = pl.BlockSpec(memory_space=pl.ANY)


def place():
    d, y = lax.axis_index("dp"), lax.axis_index("fsdp")
    return lax.div(d, 16), y, lax.rem(lax.div(d, 2), 8), lax.rem(d, 2)


def ring(i, o, n):
    return lax.rem(i + o + n, n)


def at128(i):
    return pl.multiple_of(i, 128)


def at16(i):
    return pl.multiple_of(i, 16)


def nt(a, b):
    return lax.dot_general(a, b, (((1,), (1,)), ((), ())), preferred_element_type=F32)


def tn(a, b):
    return lax.dot_general(a, b, (((0,), (0,)), ((), ())), preferred_element_type=F32)


def mm(a, b):
    return jnp.dot(a, b, preferred_element_type=F32)


def split(v):
    hi = v.astype(BF16)
    return hi, (v - hi.astype(F32)).astype(BF16)


def meet(peers):
    barrier = pltpu.get_barrier_semaphore()
    for x, y, z, c in peers:
        pl.semaphore_signal(barrier, inc=1, device_id=((x * NZ + z) * 2 + c, y), device_id_type=MESH)
    pl.semaphore_wait(barrier, len(peers))


class Net:
    def __init__(self, send, recv):
        self.send, self.recv, self.all = send, recv, []

    def put(self, src, dst, where):
        x, y, z, c = where
        k = len(self.all)
        copy = pltpu.make_async_remote_copy(
            src_ref=src,
            dst_ref=dst,
            send_sem=self.send.at[k],
            recv_sem=self.recv.at[k],
            device_id=((x * NZ + z) * 2 + c, y),
            device_id_type=MESH,
        )
        copy.start()
        self.all.append(copy)
        return copy

    def drain(self):
        for copy in self.all:
            copy.wait_send()


def landed(copies):
    for copy in copies:
        copy.wait_recv()


A_COPIES = 104


def items_kernel(
    lengths, states_h, scores, igain, vweight_h, pos_h, ugain, uweight_h, ids,
    ce, pp, posx, nxt,
    states, vweight, uweight, squares, squares_in, num, num_in, cat, ep, ep_in, pin, pback, pback_in,
    send, recv, local,
):
    x, y, z, c = place()
    low = lax.rem(z, 2)
    group = 4 * x + lax.div(z, 2)
    member, quarter = 2 * low + c, 2 * c + low
    base = z - low
    net = Net(send, recv)

    def peer(dx=0, dy=0, dz=0, dc=0):
        return ring(x, dx, NX), ring(y, dy, NY), ring(z, dz, NZ), ring(c, dc, 2)

    def mate(om, oy):
        m = ring(member, om, 4)
        return x, ring(y, oy, NY), base + lax.div(m, 2), lax.rem(m, 2)

    loads = [
        pltpu.make_async_copy(states_h, states, local.at[0]),
        pltpu.make_async_copy(uweight_h, uweight, local.at[1]),
        pltpu.make_async_copy(vweight_h, vweight, local.at[2]),
        pltpu.make_async_copy(
            pos_h.at[pl.ds(at16(16 * group), 16), pl.ds(at128(512 * y), 512)], pin.at[0], local.at[3]
        ),
        pltpu.make_async_copy(pos_h.at[:, pl.ds(at128(512 * y + 128 * x), 128)], posx.at[y], local.at[4]),
    ]
    for load in loads:
        load.start()
    offsets = [(om, oy) for om in range(4) for oy in range(4) if om or oy]
    meet(
        [mate(om, oy) for om, oy in offsets]
        + [peer(dz=o) for o in range(1, NZ)]
        + [peer(dx=o) for o in range(1, NX)]
    )

    rows16 = pl.ds(at16(16 * group), 16)
    pin_copies, posx_copies = [], []
    for o in range(1, NY):
        to = ring(y, o, NY)
        pin_copies.append(net.put(pos_h.at[rows16, pl.ds(at128(512 * to), 512)], pin.at[o], peer(dy=o)))
    next_copy = net.put(ids, nxt, peer(dy=-1))
    for o in range(1, NY):
        to = ring(y, o, NY)
        posx_copies.append(
            net.put(pos_h.at[:, pl.ds(at128(512 * to + 128 * x), 128)], posx.at[y], peer(dy=o))
        )

    loads[0].wait()
    ones = jnp.ones((8, 128), F32)
    item_row = lax.broadcasted_iota(jnp.int32, (8, 256), 0)
    sums = jnp.zeros((8, 256), F32)
    for i in range(4):
        part = jnp.zeros((256, 128), F32)
        for j in range(8):
            v = states[i, :, 128 * j:128 * (j + 1)].astype(F32)
            part = part + v * v
        hi, lo = split(part)
        low2 = (part - hi.astype(F32) - lo.astype(F32)).astype(BF16)
        ones16 = ones.astype(BF16)
        sums = jnp.where(item_row == i, nt(ones16, hi) + nt(ones16, lo) + nt(ones16, low2), sums)
    squares[...] = sums
    square_copies = [net.put(squares, squares_in.at[o - 1], peer(dy=o)) for o in range(1, NY)]

    loads[1].wait()
    loads[3].wait()
    landed(pin_copies)
    gain_part = ugain[:, pl.ds(at128(512 * y), 512)]
    pos_rows = pin[...].astype(F32).reshape(64, 512) * gain_part
    pback[...] = mm(
        pos_rows.astype(BF16), uweight[:, pl.ds(at128(512 * quarter), 512)]
    ).reshape(4, 16, 512)
    back_copies = [net.put(pback.at[o], pback_in.at[o - 1], peer(dy=-o)) for o in range(1, NY)]

    landed(square_copies)
    inv_rms = lax.rsqrt((squares[...] + squares_in[0] + squares_in[1] + squares_in[2]) / D + 1e-05)
    token = lax.broadcasted_iota(jnp.int32, (16, 256), 1)
    pooled_hi, pooled_lo = [], []
    for i in range(4):
        weights = jnp.where(token < lengths[i], jnp.exp(scores[i]), 0.0)
        weights = weights * (inv_rms[i:i + 1] / jnp.sum(weights, axis=1, keepdims=True))
        hi, lo = split(weights)
        both = mm(jnp.concatenate([hi, lo], axis=0), states[i])
        pooled = (both[:16] + both[16:]) * igain[...]
        hi, lo = split(pooled)
        pooled_hi.append(hi)
        pooled_lo.append(lo)
    left = jnp.concatenate(pooled_hi + pooled_lo, axis=0)
    loads[2].wait()
    head = lax.broadcasted_iota(jnp.int32, (4, 16, 256), 1)
    tile = lax.broadcasted_iota(jnp.int32, (4, 16, 256), 2) // 128
    for j in range(8):
        full = mm(left, vweight[:, 256 * j:256 * (j + 1)])
        full = (full[:64] + full[64:]).reshape(4, 16, 256)
        block = jnp.sum(jnp.where(head == tile + 2 * j, full, 0.0), axis=1)
        num[j // 2, 4 * (j % 2):4 * (j % 2) + 4, :] = block
    num_copies = []
    for om, oy in offsets:
        num_copies.append(net.put(num.at[ring(y, oy, NY)], num_in.at[oy, member], mate(om, oy)))
    num_in[0, pl.ds(member, 1)] = num[pl.ds(y, 1)]

    landed(back_copies)
    pp_rows, pp_cols = rows16, pl.ds(at128(512 * quarter), 512)
    pp[pp_rows, pp_cols] = (pback[0] + pback_in[0] + pback_in[1] + pback_in[2]).astype(BF16)
    own = pp.at[pp_rows, pp_cols]
    pp_z = [net.put(own, own, peer(dz=o)) for o in range(1, NZ)]

    landed(num_copies)
    for m in range(4):
        total = num_in[0, m] + num_in[1, m] + num_in[2, m] + num_in[3, m]
        cat[4 * m:4 * m + 4, :256] = total[:4]
        cat[4 * m:4 * m + 4, 256:] = total[4:]
    embed = cat[...].astype(BF16)
    gained = (embed.astype(F32) * gain_part).astype(BF16)
    for t in range(NY):
        ep[t] = mm(gained, uweight[:, pl.ds(at128(512 * t + 128 * quarter), 128)])
    ep_copies = [net.put(ep.at[ring(y, o, NY)], ep_in.at[o - 1], peer(dy=o)) for o in range(1, NY)]
    ce_cols = pl.ds(at128(512 * y + 128 * quarter), 128)
    ce[0, rows16, ce_cols] = cat[:, pl.ds(at128(128 * quarter), 128)].astype(BF16)
    block = ce.at[0, rows16, ce_cols]
    cat_z = [net.put(block, block, peer(dz=o)) for o in range(1, NZ)]

    landed(pp_z)
    own = pp.at[pl.ds(at16(64 * x), 64), pl.ds(at128(1024 * c), 1024)]
    pp_x = [net.put(own, own, peer(dx=o)) for o in range(1, NX)]

    landed(ep_copies)
    ce[1, rows16, ce_cols] = (ep[pl.ds(y, 1)][0] + ep_in[0] + ep_in[1] + ep_in[2]).astype(BF16)
    block = ce.at[1, rows16, ce_cols]
    ep_z = [net.put(block, block, peer(dz=o)) for o in range(1, NZ)]

    rows64 = pl.ds(at16(64 * x), 64)

    def cols(t):
        return pl.ds(at128(512 * t + 256 * c), 256)

    landed(cat_z)
    block = ce.at[0, rows64, cols(y)]
    cat_x = [net.put(block, block, peer(dx=o)) for o in range(1, NX)]
    landed(ep_z)
    block = ce.at[1, rows64, cols(y)]
    ep_y = [net.put(block, block, peer(dy=o)) for o in range(1, NY)]

    landed(pp_x)
    own = pp.at[:, pl.ds(at128(1024 * c), 1024)]
    final = [net.put(own, own, peer(dc=1))]

    landed(cat_x)
    block = ce.at[0, :, cols(y)]
    cat_y = [net.put(block, block, peer(dy=o)) for o in range(1, NY)]
    final.append(net.put(block, block, peer(dc=1)))
    landed(ep_y)
    ep_x = []
    for o in range(1, NX):
        for t in range(NY):
            block = ce.at[1, rows64, cols(t)]
            ep_x.append(net.put(block, block, peer(dx=o)))
    for t in range(NY):
        block = ce.at[1, rows64, cols(t)]
        final.append(net.put(block, block, peer(dc=1)))
    for o in range(1, NY):
        cat_y[o - 1].wait_recv()
        block = ce.at[0, :, cols(ring(y, -o, NY))]
        final.append(net.put(block, block, peer(dc=1)))
    for o in range(1, NX):
        landed(ep_x[4 * (o - 1):4 * o])
        for t in range(NY):
            block = ce.at[1, pl.ds(at16(64 * ring(x, -o, NX)), 64), cols(t)]
            final.append(net.put(block, block, peer(dc=1)))
    landed(final)
    landed(posx_copies)
    landed([next_copy])
    loads[4].wait()
    net.drain()


def items(lengths, states, scores, igain, vweight, pos, ugain, uweight, ids):
    return pl.pallas_call(
        items_kernel,
        out_shape=(
            jax.ShapeDtypeStruct((2, 256, HV), BF16),
            jax.ShapeDtypeStruct((256, HV), BF16),
            jax.ShapeDtypeStruct((4, 256, 128), BF16),
            jax.ShapeDtypeStruct((8, 256), jnp.int32),
        ),
        in_specs=[pl.BlockSpec(memory_space=pltpu.SMEM), ANY, VM, VM, ANY, ANY, VM, ANY, VM],
        out_specs=(VM, VM, VM, VM),
        scratch_shapes=[
            pltpu.VMEM((4, 256, 1024), BF16),
            pltpu.VMEM((1024, HV), BF16),
            pltpu.VMEM((512, HV), BF16),
            pltpu.VMEM((8, 256), F32),
            pltpu.VMEM((3, 8, 256), F32),
            pltpu.VMEM((4, 8, 256), F32),
            pltpu.VMEM((4, 4, 8, 256), F32),
            pltpu.VMEM((16, 512), F32),
            pltpu.VMEM((4, 16, 128), F32),
            pltpu.VMEM((3, 16, 128), F32),
            pltpu.VMEM((4, 16, 512), BF16),
            pltpu.VMEM((4, 16, 512), F32),
            pltpu.VMEM((3, 16, 512), F32),
            pltpu.SemaphoreType.DMA((A_COPIES,)),
            pltpu.SemaphoreType.DMA((A_COPIES,)),
            pltpu.SemaphoreType.DMA((5,)),
        ],
        compiler_params=pltpu.CompilerParams(
            collective_id=0, has_side_effects=True, vmem_limit_bytes=40 * 2**20
        ),
        name="items",
    )(lengths, states, scores, igain, vweight, pos, ugain, uweight, ids)


CHUNK = 512


def users_kernel(
    ids, targets, negs, valid, ce, pp, pos,
    s_out, q_out, r_out,
    in_v, ep_v, u_v, uh_v, ug_v, iu_v,
):
    js = [slice(j, j + CHUNK) for j in range(0, HV, CHUNK)]
    item = lax.broadcasted_iota(jnp.int32, (256, 256), 0)
    hot_t32 = (item == ids[...]).astype(F32)
    hot_t = hot_t32.astype(BF16)
    hot = hot_t32.T.astype(BF16)
    target_t = (item == targets[...]).astype(F32)
    counts = jnp.sum((item == negs[...]).astype(F32), axis=1, keepdims=True)

    squares = jnp.zeros((256, 1), F32)
    cat_squares = jnp.zeros((256, 1), F32)
    for j in js:
        v = mm(hot, ce[0, :, j]) + pos[:, j].astype(F32)
        in_v[:, j] = v
        squares += jnp.sum(v * v, axis=1, keepdims=True)
        w = ce[0, :, j].astype(F32)
        cat_squares += jnp.sum(w * w, axis=1, keepdims=True)
    inv = lax.rsqrt(squares / HV + 1e-05)
    cat_inv = 1.0 / jnp.sqrt(cat_squares + 1e-06)
    out_squares = jnp.zeros((256, 1), F32)
    for j in js:
        e = mm(hot, ce[1, :, j]) + pp[:, j].astype(F32)
        ep_v[:, j] = e
        v = in_v[:, j] + inv * e
        u_v[:, j] = v
        out_squares += jnp.sum(v * v, axis=1, keepdims=True)
    out_inv = 1.0 / jnp.sqrt(out_squares + 1e-06)
    logits = jnp.zeros((256, 256), F32)
    for j in js:
        u = u_v[:, j] * out_inv
        u_v[:, j] = u
        hi, lo = split(u)
        uh_v[:, j] = hi
        logits += nt(ce[0, :, j], hi) + nt(ce[0, :, j], lo)
    powers = jnp.exp(20.0 * cat_inv * logits)
    pos_power = jnp.sum(target_t * powers, axis=0, keepdims=True)
    total = pos_power + jnp.sum(counts * powers, axis=0, keepdims=True)
    scale = valid[...] * (1.0 / (USERS * (ULEN - 1)))
    grad_t = scale * (counts * powers / total + target_t * (pos_power / total - 1.0))
    by_item = grad_t.astype(BF16)
    by_row_hi, by_row_lo = split((grad_t * cat_inv).T)
    along = jnp.zeros((256, 1), F32)
    cat_along = jnp.zeros((256, 1), F32)
    for j in js:
        v = 20.0 * (mm(by_row_hi, ce[0, :, j]) + mm(by_row_lo, ce[0, :, j]))
        ug_v[:, j] = v
        along += jnp.sum(v * u_v[:, j], axis=1, keepdims=True)
        v = 20.0 * mm(by_item, uh_v[:, j])
        iu_v[:, j] = v
        cat_along += jnp.sum(v * ce[0, :, j].astype(F32), axis=1, keepdims=True)
    cat_along = cat_along * cat_inv * cat_inv
    inner = jnp.zeros((256, 1), F32)
    for j in js:
        g = (ug_v[:, j] - u_v[:, j] * along) * out_inv
        ug_v[:, j] = g
        inner += jnp.sum(g * ep_v[:, j], axis=1, keepdims=True)
    inner = inner * (inv * inv * inv / HV)
    for j in js:
        g = ug_v[:, j]
        q = (inv * g).astype(BF16)
        q_out[:, j] = q
        s_out[:, j] = mm(hot_t, q).astype(BF16)
        direct = (g - in_v[:, j] * inner).astype(BF16)
        item_grad = (iu_v[:, j] - ce[0, :, j].astype(F32) * cat_along) * cat_inv
        r_out[:, j] = (mm(hot_t, direct) + item_grad).astype(BF16)


def users(ids, targets, negs, valid, ce, pp, pos):
    shape = jax.ShapeDtypeStruct((256, HV), BF16)
    return pl.pallas_call(
        users_kernel,
        out_shape=(shape, shape, shape),
        in_specs=[VM] * 7,
        out_specs=(VM, VM, VM),
        scratch_shapes=[
            pltpu.VMEM((256, HV), F32),
            pltpu.VMEM((256, HV), F32),
            pltpu.VMEM((256, HV), F32),
            pltpu.VMEM((256, HV), BF16),
            pltpu.VMEM((256, HV), F32),
            pltpu.VMEM((256, HV), F32),
        ],
        compiler_params=pltpu.CompilerParams(vmem_limit_bytes=48 * 2**20),
        name="users",
    )(ids, targets, negs, valid, ce, pp, pos)


C_COPIES = 100


def grads_kernel(
    s, q, r, ce_h, posx, ugain, uweight_h,
    item_out, weight_out,
    cat, uweight,
    s1_in, q1_in, r1_in, s1, q1, r1,
    s2_in, r2_in, q2_in, s2, r2, q2,
    s3_in, r3_in, q3_in, s3, r3,
    s4_in, qg, sg, t, t_in, item,
    send, recv, local,
):
    x, y, z, c = place()
    net = Net(send, recv)

    def peer(dx=0, dy=0, dz=0, dc=0):
        return ring(x, dx, NX), ring(y, dy, NY), ring(z, dz, NZ), ring(c, dc, 2)

    zc = [(dz, dc) for dc in range(2) for dz in range(NZ) if dz or dc]
    xy = [(dx, dy) for dx in range(NX) for dy in range(NY) if dx or dy]
    loads = [
        pltpu.make_async_copy(ce_h.at[0, :, pl.ds(at128(512 * y + 128 * x), 128)], cat, local.at[0]),
        pltpu.make_async_copy(uweight_h.at[:, pl.ds(at128(1024 * c + 128 * z), 128)], uweight, local.at[1]),
    ]
    for load in loads:
        load.start()
    meet([peer(dz=dz, dc=dc) for dz, dc in zc] + [peer(dx=dx, dy=dy) for dx, dy in xy])

    mine = pl.ds(at128(1024 * c), 1024)
    theirs = pl.ds(at128(1024 * ring(c, 1, 2)), 1024)
    s_copy = net.put(s.at[:, theirs], s1_in, peer(dc=1))
    r_copy = net.put(r.at[:, ring(c, 1, 2)], r1_in, peer(dc=1))
    q_copy = net.put(q.at[:, theirs], q1_in, peer(dc=1))
    s_copy.wait_recv()
    s1[...] = (s[:, mine].astype(F32) + s1_in[...].astype(F32)).astype(BF16)
    s2_copies = [
        net.put(s1.at[pl.ds(at16(64 * ring(y, o, NY)), 64)], s2_in.at[o - 1], peer(dy=o)) for o in range(1, NY)
    ]
    r_copy.wait_recv()
    r1[...] = (r[:, pl.ds(c, 1)].reshape(4, 32, HV).astype(F32) + r1_in[...].astype(F32)).astype(BF16)
    r2_copies = [
        net.put(r1.at[:, :, pl.ds(at128(512 * ring(y, o, NY)), 512)], r2_in.at[o - 1], peer(dy=o))
        for o in range(1, NY)
    ]
    q_copy.wait_recv()
    q1[...] = (q[:, mine].astype(F32) + q1_in[...].astype(F32)).astype(BF16)
    q2_copies = [
        net.put(q1.at[pl.ds(at16(64 * ring(x, o, NX)), 64)], q2_in.at[o - 1], peer(dx=o)) for o in range(1, NX)
    ]

    def added(own, parts):
        total = own.astype(F32)
        for k in range(3):
            total = total + parts[k].astype(F32)
        return total

    landed(s2_copies)
    s2[...] = added(s1[pl.ds(at16(64 * y), 64)], s2_in).astype(BF16)
    s3_copies = [
        net.put(s2.at[pl.ds(at16(16 * ring(x, o, NX)), 16)], s3_in.at[o - 1], peer(dx=o)) for o in range(1, NX)
    ]
    landed(q2_copies)
    q2[...] = added(q1[pl.ds(at16(64 * x), 64)], q2_in).astype(BF16)
    q3_copies = [
        net.put(q2.at[:, pl.ds(at128(128 * ring(z, o, NZ)), 128)], q3_in.at[o - 1], peer(dz=o))
        for o in range(1, NZ)
    ]
    landed(r2_copies)
    r2[...] = added(r1[:, :, pl.ds(at128(512 * y), 512)], r2_in).astype(BF16)
    r3_copies = [net.put(r2.at[ring(x, o, NX)], r3_in.at[o - 1], peer(dx=o)) for o in range(1, NX)]

    landed(s3_copies)
    s3[...] = added(s2[pl.ds(at16(16 * x), 16)], s3_in).astype(BF16)
    s4_copies = [
        net.put(s3.at[:, pl.ds(at128(128 * ring(z, o, NZ)), 128)], s4_in.at[o - 1], peer(dz=o))
        for o in range(1, NZ)
    ]
    landed(q3_copies)
    total = q2[:, pl.ds(at128(128 * z), 128)].astype(F32)
    for k in range(NZ - 1):
        total = total + q3_in[k].astype(F32)
    spot = 4 * y + x
    qg[pl.ds(spot, 1)] = total.astype(BF16)[None]
    qg_copies = [net.put(qg.at[spot], qg.at[spot], peer(dx=dx, dy=dy)) for dx, dy in xy]
    landed(s4_copies)
    total = s3[:, pl.ds(at128(128 * z), 128)].astype(F32)
    for k in range(NZ - 1):
        total = total + s4_in[k].astype(F32)
    sg[pl.ds(spot, 1)] = total.astype(BF16)[None]
    sg_copies = [net.put(sg.at[spot], sg.at[spot], peer(dx=dx, dy=dy)) for dx, dy in xy]
    landed(r3_copies)
    r3[...] = added(r2[pl.ds(x, 1)][0], r3_in)

    for load in loads:
        load.wait()
    gain_rows = ugain[:, pl.ds(at128(512 * y + 128 * x), 128)]
    landed(qg_copies)
    positions = (posx[...].astype(F32).reshape(1024, 128) * gain_rows).astype(BF16)
    tile = tn(positions, qg[...].reshape(1024, 128))
    landed(sg_copies)
    embeds = (cat[...].astype(F32) * gain_rows).astype(BF16)
    tile = tile + tn(embeds, sg[...].reshape(256, 128))
    wrows = pl.ds(at16(128 * x), 128)
    wcols = pl.ds(at128(1024 * c + 128 * z), 128)
    weight_out[wrows, wcols] = tile.astype(BF16)
    block = weight_out.at[wrows, wcols]
    weight_z = [net.put(block, block, peer(dz=o)) for o in range(1, NZ)]

    back = nt(sg[pl.ds(4 * x, 4)].reshape(64, 128), uweight[...]) * ugain[:, pl.ds(at128(512 * y), 512)]
    half = lax.broadcasted_iota(jnp.int32, (64, 512), 0) // 32
    both = jnp.concatenate([r3[...], r3[...]], axis=0)
    back = back + jnp.where(half == c, both, 0.0)
    back = back.reshape(16, 4, 512)
    t[...] = jnp.concatenate([back[:, :, :256], back[:, :, 256:]], axis=1)
    t_copies = []
    for k, (dz, dc) in enumerate(zc):
        to = peer(dz=dz, dc=dc)
        t_copies.append(net.put(t.at[2 * to[2] + to[3]], t_in.at[k], to))

    landed(weight_z)
    block = weight_out.at[wrows, mine]
    weight_x = [net.put(block, block, peer(dx=o)) for o in range(1, NX)]
    final = [net.put(block, block, peer(dc=1))]

    landed(t_copies)
    total = t[pl.ds(2 * z + c, 1)][0]
    for k in range(len(zc)):
        total = total + t_in[k]
    item[pl.ds(y, 1)] = total[None]
    item_copies = [net.put(item.at[y], item.at[y], peer(dy=o)) for o in range(1, NY)]

    for o in range(1, NX):
        weight_x[o - 1].wait_recv()
        block = weight_out.at[pl.ds(at16(128 * ring(x, -o, NX)), 128), mine]
        final.append(net.put(block, block, peer(dc=1)))
    landed(item_copies)
    for k in range(NY):
        item_out[:, 512 * k:512 * k + 256] = item[k, :4]
        item_out[:, 512 * k + 256:512 * k + 512] = item[k, 4:]
    landed(final)
    net.drain()


def grads(s, q, r, ce, posx, ugain, uweight):
    return pl.pallas_call(
        grads_kernel,
        out_shape=(
            jax.ShapeDtypeStruct((4, HV), F32),
            jax.ShapeDtypeStruct((512, HV), BF16),
        ),
        in_specs=[VM, VM, VM, ANY, VM, VM, ANY],
        out_specs=(VM, VM),
        scratch_shapes=[
            pltpu.VMEM((256, 128), BF16),
            pltpu.VMEM((512, 128), BF16),
            pltpu.VMEM((256, 1024), BF16),
            pltpu.VMEM((256, 1024), BF16),
            pltpu.VMEM((4, 32, HV), BF16),
            pltpu.VMEM((256, 1024), BF16),
            pltpu.VMEM((256, 1024), BF16),
            pltpu.VMEM((4, 32, HV), BF16),
            pltpu.VMEM((3, 64, 1024), BF16),
            pltpu.VMEM((3, 4, 32, 512), BF16),
            pltpu.VMEM((3, 64, 1024), BF16),
            pltpu.VMEM((64, 1024), BF16),
            pltpu.VMEM((4, 32, 512), BF16),
            pltpu.VMEM((64, 1024), BF16),
            pltpu.VMEM((3, 16, 1024), BF16),
            pltpu.VMEM((3, 32, 512), BF16),
            pltpu.VMEM((7, 64, 128), BF16),
            pltpu.VMEM((16, 1024), BF16),
            pltpu.VMEM((32, 512), F32),
            pltpu.VMEM((7, 16, 128), BF16),
            pltpu.VMEM((16, 64, 128), BF16),
            pltpu.VMEM((16, 16, 128), BF16),
            pltpu.VMEM((16, 8, 256), F32),
            pltpu.VMEM((15, 8, 256), F32),
            pltpu.VMEM((4, 8, 256), F32),
            pltpu.SemaphoreType.DMA((C_COPIES,)),
            pltpu.SemaphoreType.DMA((C_COPIES,)),
            pltpu.SemaphoreType.DMA((2,)),
        ],
        compiler_params=pltpu.CompilerParams(
            collective_id=1, has_side_effects=True, vmem_limit_bytes=40 * 2**20
        ),
        name="grads",
    )(s, q, r.reshape(4, 2, 32, HV), ce, posx, ugain, uweight)


def local(
    item_states, item_scores, item_lengths, item_gain, value_weight,
    user_items, negatives, position_embed, user_gain, user_weight,
):
    ugain = user_gain.reshape(1, HV)
    ids = jnp.broadcast_to(user_items, (8, 256))
    ce, pp, posx, nxt = items(
        item_lengths, item_states, item_scores, item_gain.reshape(1, -1), value_weight,
        position_embed, ugain, user_weight, ids,
    )
    targets = jnp.concatenate([user_items[:, 1:], nxt[:1, :1]], axis=1)
    spots = lax.axis_index("fsdp") * 256 + jnp.arange(256)[None, :]
    valid = (spots < ULEN - 1).astype(F32)
    s, q, r = users(user_items, targets, negatives, valid, ce, pp, position_embed)
    return grads(s, q, r, ce, posx, ugain, user_weight)


def solution(mesh):
    return jax.shard_map(
        local,
        mesh=mesh,
        in_specs=(
            P("dp", None, "fsdp"), P("dp", None, None), P("dp"), P("fsdp"), P("fsdp", None),
            P("dp", "fsdp"), P("dp", None), P("fsdp", None), P(), P("fsdp", None),
        ),
        out_specs=(P("dp", None), P("fsdp", None)),
        check_vma=False,
    )
```

time: 888 us -> 122 us (0.14)
  waiting for transfers between devices: 473 us -> 0 us
  blocking collectives: 325 us -> 0 us
  Pallas kernels: 0 us -> 106 us
  matrix products: 42 us -> 0 us
  between operations: 14.8 us -> 0.73 us
    psum x4 -> x0, blocking collectives: 325 us -> none  [the longest x1 290 us: local(): weight_grad = lax.psum(weight_rows, 'dp').astype(jnp.bfloat16)]
    unnamed x5 -> x0, waiting for transfers between devices: 175 us -> none
    all_gather x2 -> x0, waiting for transfers between devices: 156 us -> none  [the longest x1 83.2 us: local(): catalog_rows = lax.all_gather(item_embed, 'dp', axis=0, tiled=True)]
    reduce_scatter x1 -> x0, waiting for transfers between devices: 139 us -> none  [local(): lax.psum_scatter(contract_first(user_normed, grad_cast), 'fsdp', scatter_...]
    pallas_call x0 -> x3, Pallas kernels: none -> 106 us  [the longest x1 51.4 us: grads(): pl.pallas_call(grads_kernel, out_shape=(jax.ShapeDtypeStruct((4, HV), F32...]
    dot_general x9 -> x0, matrix products: 42 us -> none  [the longest x4 19.3 us: contract_first(): lax.dot_general(left, right, (((0,), (0,)), ((), ())), precision=precisio...]
  transfers between devices with their start and end apart: 6 -> 0, of which waited for: 5 -> 0; matrix products, arithmetic and copies ran while one was open for 3% -> 0% of each run, Pallas kernels for 0% -> 0%
where the time goes in v1:
time: 122 us
  Pallas kernels  106 us (87%)
  local copies, waits for them, and re-layouts  14.7 us (12%)
    pallas_call x1, Pallas kernels, grads(): pl.pallas_call(grads_kernel, out_shape=(jax.ShapeDtypeStruct((4, HV), F32...  51.4 us
    pallas_call x1, Pallas kernels, items(): pl.pallas_call(items_kernel, out_shape=(jax.ShapeDtypeStruct((2, 256, HV)...  47 us
    unnamed x32, local copies, waits for them, and re-layouts  12.7 us
    pallas_call x1, Pallas kernels, users(): pl.pallas_call(users_kernel, out_shape=(shape, shape, shape), in_specs=[V...  7.4 us

profile of v1, /device:TPU:1, one launch (start us, length us, event | category | flops | bytes accessed | tf_op | source)
XLA Modules:
  0.0 121.9 jit_solution(16784954343841928060)
XLA Ops:
  0.6 0.8 slice.6
  1.4 0.7 broadcast_in_dim.9.ids
  2.1 0.0 copy-start.2
  2.1 1.6 %copy-done.2 = bf16[512,2048]{1,0:T(8,128)(2,1)S(1)} copy-done((bf16[512,2048]{1,0:T(8,128)(2,1)S(1)}, bf16[512,2048]{1,0:T(8,128)(2,1)}, u32[]{:S(2)}) %copy-start.2) | copy-done | bytes 2097176
  3.7 0.0 copy-start.4
  3.7 1.2 %copy-done.4 = bf16[256,2048]{1,0:T(8,128)(2,1)S(1)} copy-done((bf16[256,2048]{1,0:T(8,128)(2,1)S(1)}, bf16[256,2048]{1,0:T(8,128)(2,1)}, u32[]{:S(2)}) %copy-start.4) | copy-done | bytes 1048600
  4.9 0.0 copy-start.6
  4.9 2.2 %copy-done.6 = bf16[1024,2048]{1,0:T(8,128)(2,1)S(1)} copy-done((bf16[1024,2048]{1,0:T(8,128)(2,1)S(1)}, bf16[1024,2048]{1,0:T(8,128)(2,1)}, u32[]{:S(2)}) %copy-start.6) | copy-done | bytes 4194328
  7.1 0.0 copy-start.7
  7.1 1.6 %copy-done.7 = bf16[4,256,1024]{2,1,0:T(8,128)(2,1)S(1)} copy-done((bf16[4,256,1024]{2,1,0:T(8,128)(2,1)S(1)}, bf16[4,256,1024]{2,1,0:T(8,128)(2,1)}, u32[]{:S(2)}) %copy-start.7) | copy-done | bytes 2097176
  8.7 0.0 copy-start.8
  8.7 0.8 copy-done.8
  9.5 0.0 copy-start.9
  9.5 0.7 copy-done.9
  10.2 0.0 copy-start.12
  10.2 0.7 copy-done.12
  10.9 0.0 copy-start.14
  10.9 0.7 copy-done.14
  11.6 0.0 copy-start.5
  11.6 0.0 copy-start.11
  11.6 0.0 copy-start.13
  11.6 47.0 %items.1 = (bf16[2,256,2048]{2,1,0:T(8,128)(2,1)S(1)}, bf16[256,2048]{1,0:T(8,128)(2,1)S(1)}, bf16[4,256,128]{2,1,0:T(8,128)(2,1)S(1)}, s32[8,256]{1,0:T(8,128)S(1)}) custom-call(s32[4]{0:T(128)S(1)} %copy-done.14, bf16[4,256,1024]{2,1,0:T(8,128)(2,1)S(1)} %copy-done.7, f32[4,16,256]{2,1,0:T(8,128)S(1)} %copy-done.8, f32[1,1024]{1,0:T(1,128)S(1)} %bitcast.8, ...), custom_call_target="tpu_custom_call" | custom-call | tf_op jit(solution)/shard_map/items/pallas_call | solution.py:268
  58.6 0.0 copy-start
  58.6 1.3 %copy-done = bf16[2,256,2048]{2,1,0:T(8,128)(2,1)} copy-done((bf16[2,256,2048]{2,1,0:T(8,128)(2,1)}, bf16[2,256,2048]{2,1,0:T(8,128)(2,1)S(1)}, u32[]{:S(2)}) %copy-start) | copy-done | bytes 2097176
  59.9 0.5 slice.7
  60.4 0.7 pad_add_fusion.targets
  61.1 0.0 copy-done.5
  61.1 0.0 copy-done.11
  61.1 0.0 copy-done.13
  61.1 0.0 copy-start.1
  61.2 0.0 copy-start.3
  61.2 0.0 copy-start.10
  61.2 7.4 %users.1 = (bf16[256,2048]{1,0:T(8,128)(2,1)S(1)}, bf16[256,2048]{1,0:T(8,128)(2,1)S(1)}, bf16[256,2048]{1,0:T(8,128)(2,1)S(1)}) custom-call(s32[1,256]{1,0:T(1,128)S(1)} %copy-done.11, s32[1,256]{1,0:T(1,128)S(1)} %pad_add_fusion.targets, s32[1,256]{1,0:T(1,128)S(1)} %copy-done.13, f32[1,256]{1,0:T(1,128)S(1)} %compare_convert_fusion.valid, ...), custom_call_target="tpu_custom_call" | custom-call | tf_op jit(solution)/shard_map/users/pallas_call | solution.py:379
  68.6 0.0 copy-done.1
  68.6 0.0 copy-done.3
  68.6 0.0 copy-done.10
  68.6 51.4 %grads.1 = (f32[4,2048]{1,0:T(4,128)S(1)}, bf16[512,2048]{1,0:T(8,128)(2,1)S(1)}) custom-call(bf16[256,2048]{1,0:T(8,128)(2,1)S(1)} %get-tuple-element.12.s, bf16[256,2048]{1,0:T(8,128)(2,1)S(1)} %get-tuple-element.13.q, bf16[4,2,32,2048]{3,2,1,0:T(8,128)(2,1)S(1)} %bitcast.4, bf16[2,256,2048]{2,1,0:T(8,128)(2,1)S(1)} %copy-done.1, ...), custom_call_target="tpu_custom_call" | custom-call | tf_op jit(solution)/shard_map/grads/pallas_call | solution.py:542
  120.0 0.6 copy.14
  120.6 1.3 %copy.15 = bf16[512,2048]{1,0:T(8,128)(2,1)} copy(bf16[512,2048]{1,0:T(8,128)(2,1)S(1)} %get-tuple-element.19) | data formatting | bytes 4194304
  (1 shorter events, 0.0 us)
Async XLA Ops:
  2.1 1.6 %copy-start.2 = (bf16[512,2048]{1,0:T(8,128)(2,1)S(1)}, bf16[512,2048]{1,0:T(8,128)(2,1)}, u32[]{:S(2)}) copy-start(bf16[512,2048]{1,0:T(8,128)(2,1)} %uweight_h.3) | copy-start | bytes 6291460
  3.7 1.2 %copy-start.4 = (bf16[256,2048]{1,0:T(8,128)(2,1)S(1)}, bf16[256,2048]{1,0:T(8,128)(2,1)}, u32[]{:S(2)}) copy-start(bf16[256,2048]{1,0:T(8,128)(2,1)} %pos.1) | copy-start | bytes 3145732
  4.9 2.2 %copy-start.6 = (bf16[1024,2048]{1,0:T(8,128)(2,1)S(1)}, bf16[1024,2048]{1,0:T(8,128)(2,1)}, u32[]{:S(2)}) copy-start(bf16[1024,2048]{1,0:T(8,128)(2,1)} %vweight_h.1) | copy-start | bytes 12582916
  7.1 1.6 %copy-start.7 = (bf16[4,256,1024]{2,1,0:T(8,128)(2,1)S(1)}, bf16[4,256,1024]{2,1,0:T(8,128)(2,1)}, u32[]{:S(2)}) copy-start(bf16[4,256,1024]{2,1,0:T(8,128)(2,1)} %states_h.1) | copy-start | bytes 6291460
  8.7 0.8 copy-start.8
  9.5 0.7 copy-start.9
  10.2 0.7 copy-start.12
  10.9 0.7 copy-start.14
  11.6 49.6 %copy-start.5 = (bf16[256,2048]{1,0:T(8,128)(2,1)S(1)}, bf16[256,2048]{1,0:T(8,128)(2,1)}, u32[]{:S(2)}) copy-start(bf16[256,2048]{1,0:T(8,128)(2,1)} %pos.1) | copy-start | bytes 3145732
  11.6 49.6 %copy-start.11 = (s32[1,256]{1,0:T(1,128)S(1)}, s32[1,256]{1,0:T(1,128)}, u32[]{:S(2)}) copy-start(s32[1,256]{1,0:T(1,128)} %ids.1) | copy-start | bytes 3076
  11.6 49.6 %copy-start.13 = (s32[1,256]{1,0:T(1,128)S(1)}, s32[1,256]{1,0:T(1,128)}, u32[]{:S(2)}) copy-start(s32[1,256]{1,0:T(1,128)} %negs.1) | copy-start | bytes 3076
  58.6 1.3 %copy-start = (bf16[2,256,2048]{2,1,0:T(8,128)(2,1)}, bf16[2,256,2048]{2,1,0:T(8,128)(2,1)S(1)}, u32[]{:S(2)}) copy-start(bf16[2,256,2048]{2,1,0:T(8,128)(2,1)S(1)} %get-tuple-element.10.ce.ce_h) | copy-start | bytes 6291460
  61.1 7.4 %copy-start.1 = (bf16[2,256,2048]{2,1,0:T(8,128)(2,1)S(1)}, bf16[2,256,2048]{2,1,0:T(8,128)(2,1)}, u32[]{:S(2)}) copy-start(bf16[2,256,2048]{2,1,0:T(8,128)(2,1)} %copy-done) | copy-start | bytes 6291460
  61.2 7.4 %copy-start.3 = (bf16[512,2048]{1,0:T(8,128)(2,1)S(1)}, bf16[512,2048]{1,0:T(8,128)(2,1)}, u32[]{:S(2)}) copy-start(bf16[512,2048]{1,0:T(8,128)(2,1)} %uweight_h.3) | copy-start | bytes 6291460
  61.2 7.4 %copy-start.10 = (f32[2048]{0:T(1024)S(1)}, f32[2048]{0:T(1024)}, u32[]{:S(2)}) copy-start(f32[2048]{0:T(1024)} %param.18) | copy-start | bytes 24580

commit v2 on v1

v2 whole, which is shorter than its diff:
```python
import jax
import jax.numpy as jnp
from jax import lax
from jax.experimental import pallas as pl
from jax.experimental.pallas import tpu as pltpu
from jax.sharding import PartitionSpec as P

MESH = pl.DeviceIdType.MESH
F32, BF16 = jnp.float32, jnp.bfloat16
NX, NY, NZ = 4, 4, 8
D, HV, ULEN, USERS = 4096, 2048, 1024, 64
TILES, CHUNK = 4, 512
VM = pl.BlockSpec(memory_space=pltpu.VMEM)
ANY = pl.BlockSpec(memory_space=pl.ANY)
COPIES = 208


def place():
    d, y = lax.axis_index("dp"), lax.axis_index("fsdp")
    return lax.div(d, 16), y, lax.rem(lax.div(d, 2), 8), lax.rem(d, 2)


def ring(i, o, n):
    return lax.rem(i + o + n, n)


def at128(i):
    return pl.multiple_of(i, 128)


def at16(i):
    return pl.multiple_of(i, 16)


def nt(a, b):
    return lax.dot_general(a, b, (((1,), (1,)), ((), ())), preferred_element_type=F32)


def tn(a, b):
    return lax.dot_general(a, b, (((0,), (0,)), ((), ())), preferred_element_type=F32)


def mm(a, b):
    return jnp.dot(a, b, preferred_element_type=F32)


def split(v):
    hi = v.astype(BF16)
    return hi, (v - hi.astype(F32)).astype(BF16)


def meet(peers):
    barrier = pltpu.get_barrier_semaphore()
    for x, y, z, c in peers:
        pl.semaphore_signal(barrier, inc=1, device_id=((x * NZ + z) * 2 + c, y), device_id_type=MESH)
    pl.semaphore_wait(barrier, len(peers))


class Net:
    def __init__(self, send, recv):
        self.send, self.recv, self.all = send, recv, []

    def put(self, src, dst, where):
        x, y, z, c = where
        k = len(self.all)
        assert k < COPIES
        copy = pltpu.make_async_remote_copy(
            src_ref=src,
            dst_ref=dst,
            send_sem=self.send.at[k],
            recv_sem=self.recv.at[k],
            device_id=((x * NZ + z) * 2 + c, y),
            device_id_type=MESH,
        )
        copy.start()
        self.all.append(copy)
        return copy

    def drain(self):
        for copy in self.all:
            copy.wait_send()


def landed(copies):
    for copy in copies:
        copy.wait_recv()


def added(own, parts, count):
    total = own.astype(F32)
    for k in range(count):
        total = total + parts[k].astype(F32)
    return total


def whole_kernel(
    lengths, states_h, scores_h, igain, vweight_h, pos_h, ugain, uweight_h, ids, negs,
    item_out, weight_out,
    states, scores, vweight, uweight, pos, ids8,
    squares, squares_in, num, num_in, cat, ep, ep_in, pin, pback, pback_in, posx, nxt, ce, pp,
    in_v, ep_v, u_v, uh_v, ug_v, iu_v,
    s, q, r, s1_in, q1_in, r1_in, s1, q1, r1, s2_in, r2_in, q2_in, s2, r2, q2, s3_in, r3_in, q3_in, s3, s4_in,
    qg, sg, t, t_in, item,
    send, recv, local,
):
    x, y, z, c = place()
    low = lax.rem(z, 2)
    group = 4 * x + lax.div(z, 2)
    member, quarter = 2 * low + c, 2 * c + low
    base = z - low
    net = Net(send, recv)

    def peer(dx=0, dy=0, dz=0, dc=0):
        return ring(x, dx, NX), ring(y, dy, NY), ring(z, dz, NZ), ring(c, dc, 2)

    def mate(om, oy):
        m = ring(member, om, 4)
        return x, ring(y, oy, NY), base + lax.div(m, 2), lax.rem(m, 2)

    rows16, rows64 = pl.ds(at16(16 * group), 16), pl.ds(at16(64 * x), 64)
    mine, theirs = pl.ds(at128(256 * c), 256), pl.ds(at128(256 * ring(c, 1, 2)), 256)
    own512 = pl.ds(at128(512 * y), 512)
    loads = [
        pltpu.make_async_copy(states_h, states, local.at[0]),
        pltpu.make_async_copy(pos_h.at[rows16, own512], pin.at[0], local.at[1]),
        pltpu.make_async_copy(uweight_h, uweight, local.at[2]),
        pltpu.make_async_copy(scores_h, scores, local.at[3]),
        pltpu.make_async_copy(vweight_h, vweight, local.at[4]),
        pltpu.make_async_copy(pos_h.at[:, pl.ds(at128(512 * y + 128 * x), 128)], posx.at[y], local.at[5]),
        pltpu.make_async_copy(pos_h, pos, local.at[6]),
    ]
    for load in loads:
        load.start()
    ids8[...] = jnp.broadcast_to(ids[...], (8, 256))
    offsets = [(om, oy) for om in range(4) for oy in range(4) if om or oy]
    zs, xs, ys = range(1, NZ), range(1, NX), range(1, NY)
    zc = [(dz, dc) for dc in range(2) for dz in range(NZ) if dz or dc]
    xy = [(dx, dy) for dx in range(NX) for dy in range(NY) if dx or dy]
    meet(
        [mate(om, oy) for om, oy in offsets]
        + [peer(dz=dz, dc=dc) for dz, dc in zc]
        + [peer(dx=dx, dy=dy) for dx, dy in xy]
    )

    pin_copies = [
        net.put(pos_h.at[rows16, pl.ds(at128(512 * ring(y, o, NY)), 512)], pin.at[o], peer(dy=o)) for o in ys
    ]

    loads[0].wait()
    ones = jnp.ones((8, 128), BF16)
    item_row = lax.broadcasted_iota(jnp.int32, (8, 256), 0)
    sums = jnp.zeros((8, 256), F32)
    for i in range(4):
        part = jnp.zeros((256, 128), F32)
        for j in range(8):
            v = states[i, :, 128 * j:128 * (j + 1)].astype(F32)
            part = part + v * v
        hi, lo = split(part)
        rest = (part - hi.astype(F32) - lo.astype(F32)).astype(BF16)
        sums = jnp.where(item_row == i, nt(ones, hi) + nt(ones, lo) + nt(ones, rest), sums)
    squares[...] = sums
    square_copies = [net.put(squares, squares_in.at[o - 1], peer(dy=o)) for o in ys]

    loads[1].wait()
    loads[2].wait()
    landed(pin_copies)
    gain_part = ugain[:, own512]
    pos_rows = pin[...].astype(F32).reshape(64, 512) * gain_part
    pback[...] = mm(
        pos_rows.astype(BF16), uweight[:, pl.ds(at128(512 * quarter), 512)]
    ).reshape(4, 16, 512)
    back_copies = [net.put(pback.at[o], pback_in.at[o - 1], peer(dy=-o)) for o in ys]

    loads[3].wait()
    landed(square_copies)
    inv_rms = lax.rsqrt((squares[...] + squares_in[0] + squares_in[1] + squares_in[2]) / D + 1e-05)
    token = lax.broadcasted_iota(jnp.int32, (16, 256), 1)
    pooled_hi, pooled_lo = [], []
    for i in range(4):
        weights = jnp.where(token < lengths[i], jnp.exp(scores[i]), 0.0)
        weights = weights * (inv_rms[i:i + 1] / jnp.sum(weights, axis=1, keepdims=True))
        hi, lo = split(weights)
        both = mm(jnp.concatenate([hi, lo], axis=0), states[i])
        pooled = (both[:16] + both[16:]) * igain[...]
        hi, lo = split(pooled)
        pooled_hi.append(hi)
        pooled_lo.append(lo)
    left = jnp.concatenate(pooled_hi + pooled_lo, axis=0)
    loads[4].wait()
    head = lax.broadcasted_iota(jnp.int32, (4, 16, 256), 1)
    tile = lax.broadcasted_iota(jnp.int32, (4, 16, 256), 2) // 128
    for j in range(8):
        full = mm(left, vweight[:, 256 * j:256 * (j + 1)])
        full = (full[:64] + full[64:]).reshape(4, 16, 256)
        block = jnp.sum(jnp.where(head == tile + 2 * j, full, 0.0), axis=1)
        num[j // 2, 4 * (j % 2):4 * (j % 2) + 4, :] = block
    num_copies = []
    for om, oy in offsets:
        num_copies.append(net.put(num.at[ring(y, oy, NY)], num_in.at[oy, member], mate(om, oy)))
    num_in[0, pl.ds(member, 1)] = num[pl.ds(y, 1)]

    landed(back_copies)
    pp[pl.ds(quarter, 1), rows16] = (pback[0] + pback_in[0] + pback_in[1] + pback_in[2]).astype(BF16)[None]
    own = pp.at[quarter, rows16]
    pp_z = [net.put(own, own, peer(dz=o)) for o in zs]

    landed(num_copies)
    for m in range(4):
        total = num_in[0, m] + num_in[1, m] + num_in[2, m] + num_in[3, m]
        cat[4 * m:4 * m + 4, :256] = total[:4]
        cat[4 * m:4 * m + 4, 256:] = total[4:]
    embed = cat[...].astype(BF16)
    gained = (embed.astype(F32) * gain_part).astype(BF16)
    for k in range(NY):
        ep[k] = mm(gained, uweight[:, pl.ds(at128(512 * k + 128 * quarter), 128)])
    ep_copies = [net.put(ep.at[ring(y, o, NY)], ep_in.at[o - 1], peer(dy=o)) for o in ys]
    part = pl.ds(at128(128 * quarter), 128)
    ce[0, pl.ds(y, 1), rows16, part] = cat[:, part].astype(BF16)[None]
    block = ce.at[0, y, rows16, part]
    cat_z = [net.put(block, block, peer(dz=o)) for o in zs]

    landed(pp_z)
    own = pp.at[pl.ds(2 * c, 2), rows64]
    pp_x = [net.put(own, own, peer(dx=o)) for o in xs]

    landed(ep_copies)
    ce[1, pl.ds(y, 1), rows16, part] = (ep[pl.ds(y, 1)] + ep_in[0] + ep_in[1] + ep_in[2]).astype(BF16)
    block = ce.at[1, y, rows16, part]
    ep_z = [net.put(block, block, peer(dz=o)) for o in zs]

    landed(cat_z)
    block = ce.at[0, y, rows64, mine]
    cat_x = [net.put(block, block, peer(dx=o)) for o in xs]
    landed(ep_z)
    block = ce.at[1, y, rows64, mine]
    ep_y = [net.put(block, block, peer(dy=o)) for o in ys]

    landed(pp_x)
    own = pp.at[pl.ds(2 * c, 2)]
    final = [net.put(own, own, peer(dc=1))]

    landed(cat_x)
    block = ce.at[0, y, :, mine]
    cat_y = [net.put(block, block, peer(dy=o)) for o in ys]
    final.append(net.put(block, block, peer(dc=1)))
    landed(ep_y)
    block = ce.at[1, :, rows64, mine]
    ep_x = [net.put(block, block, peer(dx=o)) for o in xs]
    final.append(net.put(block, block, peer(dc=1)))
    for o in ys:
        cat_y[o - 1].wait_recv()
        block = ce.at[0, ring(y, -o, NY), :, mine]
        final.append(net.put(block, block, peer(dc=1)))
    for o in xs:
        ep_x[o - 1].wait_recv()
        block = ce.at[1, :, pl.ds(at16(64 * ring(x, -o, NX)), 64), mine]
        final.append(net.put(block, block, peer(dc=1)))
    next_copy = net.put(ids8, nxt, peer(dy=-1))
    posx_copies = [
        net.put(pos_h.at[:, pl.ds(at128(512 * ring(y, o, NY) + 128 * x), 128)], posx.at[y], peer(dy=o)) for o in ys
    ]
    landed(final)
    landed([next_copy])
    loads[6].wait()

    js = [slice(CHUNK * k, CHUNK * (k + 1)) for k in range(TILES)]
    all_items = lax.broadcasted_iota(jnp.int32, (256, 256), 0)
    hot_t32 = (all_items == ids[...]).astype(F32)
    hot_t = hot_t32.astype(BF16)
    hot = hot_t32.T.astype(BF16)
    lane = lax.broadcasted_iota(jnp.int32, (8, 256), 1)
    targets = jnp.where(lane == 255, pltpu.roll(nxt[...], 255, 1), pltpu.roll(ids8[...], 255, 1))[:1]
    target_t = (all_items == targets).astype(F32)
    counts = jnp.sum((all_items == negs[...]).astype(F32), axis=1, keepdims=True)
    spots = y * 256 + lax.broadcasted_iota(jnp.int32, (1, 256), 1)
    scale = jnp.where(spots < ULEN - 1, 1.0 / (USERS * (ULEN - 1)), 0.0)

    in_squares = jnp.zeros((256, 1), F32)
    cat_squares = jnp.zeros((256, 1), F32)
    for k, j in enumerate(js):
        v = mm(hot, ce[0, k]) + pos[:, j].astype(F32)
        in_v[:, j] = v
        in_squares += jnp.sum(v * v, axis=1, keepdims=True)
        w = ce[0, k].astype(F32)
        cat_squares += jnp.sum(w * w, axis=1, keepdims=True)
    inv = lax.rsqrt(in_squares / HV + 1e-05)
    cat_inv = 1.0 / jnp.sqrt(cat_squares + 1e-06)
    out_squares = jnp.zeros((256, 1), F32)
    for k, j in enumerate(js):
        e = mm(hot, ce[1, k]) + pp[k].astype(F32)
        ep_v[:, j] = e
        v = in_v[:, j] + inv * e
        u_v[:, j] = v
        out_squares += jnp.sum(v * v, axis=1, keepdims=True)
    out_inv = 1.0 / jnp.sqrt(out_squares + 1e-06)
    logits = jnp.zeros((256, 256), F32)
    for k, j in enumerate(js):
        u = u_v[:, j] * out_inv
        u_v[:, j] = u
        hi, lo = split(u)
        uh_v[:, j] = hi
        logits += nt(ce[0, k], hi) + nt(ce[0, k], lo)
    powers = jnp.exp(20.0 * cat_inv * logits)
    pos_power = jnp.sum(target_t * powers, axis=0, keepdims=True)
    total = pos_power + jnp.sum(counts * powers, axis=0, keepdims=True)
    grad_t = scale * (counts * powers / total + target_t * (pos_power / total - 1.0))
    by_item = grad_t.astype(BF16)
    by_row_hi, by_row_lo = split((grad_t * cat_inv).T)
    along = jnp.zeros((256, 1), F32)
    cat_along = jnp.zeros((256, 1), F32)
    for k, j in enumerate(js):
        v = 20.0 * (mm(by_row_hi, ce[0, k]) + mm(by_row_lo, ce[0, k]))
        ug_v[:, j] = v
        along += jnp.sum(v * u_v[:, j], axis=1, keepdims=True)
        v = 20.0 * mm(by_item, uh_v[:, j])
        iu_v[:, j] = v
        cat_along += jnp.sum(v * ce[0, k].astype(F32), axis=1, keepdims=True)
    cat_along = cat_along * cat_inv * cat_inv
    inner = jnp.zeros((256, 1), F32)
    for j in js:
        g = (ug_v[:, j] - u_v[:, j] * along) * out_inv
        ug_v[:, j] = g
        inner += jnp.sum(g * ep_v[:, j], axis=1, keepdims=True)
    inner = inner * (inv * inv * inv / HV)
    s1_copies, q1_copies, r1_copies = [], [], []
    for k, j in enumerate(js):
        g = ug_v[:, j]
        rows = (inv * g).astype(BF16)
        q[k] = rows
        q1_copies.append(net.put(q.at[k, :, theirs], q1_in.at[k], peer(dc=1)))
        s[k] = mm(hot_t, rows).astype(BF16)
        s1_copies.append(net.put(s.at[k, :, theirs], s1_in.at[k], peer(dc=1)))
        direct = (g - in_v[:, j] * inner).astype(BF16)
        item_grad = (iu_v[:, j] - ce[0, k].astype(F32) * cat_along) * cat_inv
        r[k] = (mm(hot_t, direct) + item_grad).astype(BF16)
        r1_copies.append(net.put(r.at[k, :, theirs], r1_in.at[k], peer(dc=1)))

    for k in range(TILES):
        q1_copies[k].wait_recv()
        q1[k] = (q[k, :, mine].astype(F32) + q1_in[k].astype(F32)).astype(BF16)
        s1_copies[k].wait_recv()
        s1[k] = (s[k, :, mine].astype(F32) + s1_in[k].astype(F32)).astype(BF16)
        r1_copies[k].wait_recv()
        r1[k] = (r[k, :, mine].astype(F32) + r1_in[k].astype(F32)).astype(BF16)
    s2_copies = [net.put(s1.at[:, pl.ds(at16(64 * ring(y, o, NY)), 64)], s2_in.at[o - 1], peer(dy=o)) for o in ys]
    q2_copies = [net.put(q1.at[:, pl.ds(at16(64 * ring(x, o, NX)), 64)], q2_in.at[o - 1], peer(dx=o)) for o in xs]
    r2_copies = [net.put(r1.at[ring(y, o, NY)], r2_in.at[o - 1], peer(dy=o)) for o in ys]

    landed(s2_copies)
    s2[...] = added(s1[:, pl.ds(at16(64 * y), 64)], s2_in, 3).astype(BF16)
    s3_copies = [net.put(s2.at[:, pl.ds(at16(16 * ring(x, o, NX)), 16)], s3_in.at[o - 1], peer(dx=o)) for o in xs]
    landed(q2_copies)
    q2[...] = added(q1[:, rows64], q2_in, 3).astype(BF16)

    def slot(to):
        return lax.div(to, 2), pl.ds(at128(128 * lax.rem(to, 2)), 128)

    q3_copies = []
    for o in zs:
        k, part = slot(ring(z, o, NZ))
        q3_copies.append(net.put(q2.at[k, :, part], q3_in.at[o - 1], peer(dz=o)))
    landed(r2_copies)
    r2[...] = added(r1[pl.ds(y, 1)][0], r2_in, 3).astype(BF16)
    r3_copies = [net.put(r2.at[pl.ds(at16(64 * ring(x, o, NX)), 64)], r3_in.at[o - 1], peer(dx=o)) for o in xs]
    landed(s3_copies)
    s3[...] = added(s2[:, pl.ds(at16(16 * x), 16)], s3_in, 3).astype(BF16)
    s4_copies = []
    for o in zs:
        k, part = slot(ring(z, o, NZ))
        s4_copies.append(net.put(s3.at[k, :, part], s4_in.at[o - 1], peer(dz=o)))
    spot = 4 * y + x
    own, part = slot(z)
    landed(q3_copies)
    qg[pl.ds(spot, 1)] = added(q2[pl.ds(own, 1), :, part][0], q3_in, NZ - 1).astype(BF16)[None]
    qg_copies = [net.put(qg.at[spot], qg.at[spot], peer(dx=dx, dy=dy)) for dx, dy in xy]
    landed(s4_copies)
    sg[pl.ds(spot, 1)] = added(s3[pl.ds(own, 1), :, part][0], s4_in, NZ - 1).astype(BF16)[None]
    sg_copies = [net.put(sg.at[spot], sg.at[spot], peer(dx=dx, dy=dy)) for dx, dy in xy]
    landed(r3_copies)
    r3 = added(r2[rows64], r3_in, 3)

    gain_rows = ugain[:, pl.ds(at128(512 * y + 128 * x), 128)]
    loads[5].wait()
    landed(posx_copies)
    positions = (posx[...].astype(F32).reshape(1024, 128) * gain_rows).astype(BF16)
    embeds = (ce[0, pl.ds(y, 1), :, pl.ds(at128(128 * x), 128)][0].astype(F32) * gain_rows).astype(BF16)
    landed(qg_copies)
    tile = tn(positions, qg[...].reshape(1024, 128))
    landed(sg_copies)
    tile = tile + tn(embeds, sg[...].reshape(256, 128))
    wrows = pl.ds(at16(128 * x), 128)
    zcols = pl.ds(at128(512 * lax.div(z, 2) + 256 * c + 128 * low), 128)
    weight_out[wrows, zcols] = tile.astype(BF16)
    block = weight_out.at[wrows, zcols]
    weight_z = [net.put(block, block, peer(dz=o)) for o in zs]

    back = nt(sg[pl.ds(4 * x, 4)].reshape(64, 128), uweight[:, zcols]) * gain_part
    half = lax.broadcasted_iota(jnp.int32, (64, 512), 1) // 256
    back = back + jnp.where(half == c, jnp.concatenate([r3, r3], axis=1), 0.0)
    back = back.reshape(16, 4, 512)
    t[...] = jnp.concatenate([back[:, :, :256], back[:, :, 256:]], axis=1)
    t_copies = []
    for k, (dz, dc) in enumerate(zc):
        to = peer(dz=dz, dc=dc)
        t_copies.append(net.put(t.at[2 * to[2] + to[3]], t_in.at[k], to))

    landed(weight_z)
    weight_x, final = [], []
    for k in range(TILES):
        block = weight_out.at[wrows, pl.ds(at128(512 * k + 256 * c), 256)]
        weight_x.append([net.put(block, block, peer(dx=o)) for o in xs])
        final.append(net.put(block, block, peer(dc=1)))

    landed(t_copies)
    total = added(t[pl.ds(2 * z + c, 1)][0], t_in, len(zc))
    item[pl.ds(y, 1)] = total[None]
    item_copies = [net.put(item.at[y], item.at[y], peer(dy=o)) for o in ys]

    for k in range(TILES):
        for o in xs:
            weight_x[k][o - 1].wait_recv()
            rows = pl.ds(at16(128 * ring(x, -o, NX)), 128)
            block = weight_out.at[rows, pl.ds(at128(512 * k + 256 * c), 256)]
            final.append(net.put(block, block, peer(dc=1)))
    landed(item_copies)
    for k in range(NY):
        item_out[:, 512 * k:512 * k + 256] = item[k, :4]
        item_out[:, 512 * k + 256:512 * k + 512] = item[k, 4:]
    landed(final)
    net.drain()


def local(
    item_states, item_scores, item_lengths, item_gain, value_weight,
    user_items, negatives, position_embed, user_gain, user_weight,
):
    def vm(*shape, dtype=BF16):
        return pltpu.VMEM(shape, dtype)

    return pl.pallas_call(
        whole_kernel,
        out_shape=(vm(4, HV, dtype=F32), vm(512, HV)),
        in_specs=[pl.BlockSpec(memory_space=pltpu.SMEM), ANY, ANY, VM, ANY, ANY, VM, ANY, VM, VM],
        out_specs=(VM, VM),
        scratch_shapes=[
            vm(4, 256, 1024), vm(4, 16, 256, dtype=F32), vm(1024, HV), vm(512, HV), vm(256, HV),
            vm(8, 256, dtype=jnp.int32),
            vm(8, 256, dtype=F32), vm(3, 8, 256, dtype=F32),
            vm(4, 8, 256, dtype=F32), vm(4, 4, 8, 256, dtype=F32), vm(16, 512, dtype=F32),
            vm(4, 16, 128, dtype=F32), vm(3, 16, 128, dtype=F32),
            vm(4, 16, 512), vm(4, 16, 512, dtype=F32), vm(3, 16, 512, dtype=F32),
            vm(4, 256, 128), vm(8, 256, dtype=jnp.int32),
            vm(2, 4, 256, 512), vm(4, 256, 512),
            vm(256, HV, dtype=F32), vm(256, HV, dtype=F32), vm(256, HV, dtype=F32), vm(256, HV),
            vm(256, HV, dtype=F32), vm(256, HV, dtype=F32),
            vm(4, 256, 512), vm(4, 256, 512), vm(4, 256, 512),
            vm(4, 256, 256), vm(4, 256, 256), vm(4, 256, 256),
            vm(4, 256, 256), vm(4, 256, 256), vm(4, 256, 256),
            vm(3, 4, 64, 256), vm(3, 256, 256), vm(3, 4, 64, 256),
            vm(4, 64, 256), vm(256, 256), vm(4, 64, 256),
            vm(3, 4, 16, 256), vm(3, 64, 256), vm(7, 64, 128),
            vm(4, 16, 256), vm(7, 16, 128),
            vm(16, 64, 128), vm(16, 16, 128),
            vm(16, 8, 256, dtype=F32), vm(15, 8, 256, dtype=F32), vm(4, 8, 256, dtype=F32),
            pltpu.SemaphoreType.DMA((COPIES,)),
            pltpu.SemaphoreType.DMA((COPIES,)),
            pltpu.SemaphoreType.DMA((7,)),
        ],
        compiler_params=pltpu.CompilerParams(
            collective_id=0, has_side_effects=True, vmem_limit_bytes=60 * 2**20
        ),
        name="whole",
    )(
        item_lengths, item_states, item_scores, item_gain.reshape(1, -1), value_weight,
        position_embed, user_gain.reshape(1, HV), user_weight, user_items, negatives,
    )


def solution(mesh):
    return jax.shard_map(
        local,
        mesh=mesh,
        in_specs=(
            P("dp", None, "fsdp"), P("dp", None, None), P("dp"), P("fsdp"), P("fsdp", None),
            P("dp", "fsdp"), P("dp", None), P("fsdp", None), P(), P("fsdp", None),
        ),
        out_specs=(P("dp", None), P("fsdp", None)),
        check_vma=False,
    )
```

time: 122 us -> 105 us (0.86)
  local copies, waits for them, and re-layouts: 14.7 us -> 1.94 us
  Pallas kernels: 106 us -> 102 us
    unnamed x32 -> x2, local copies, waits for them, and re-layouts: 12.7 us -> 1.94 us
    pallas_call x3 -> x1, Pallas kernels: 106 us -> 102 us  [local(): pl.pallas_call(whole_kernel, out_shape=(vm(4, HV, dtype=F32), vm(512, HV)...]
    slice x2 -> x0, local copies, waits for them, and re-layouts: 1.26 us -> none  [local(): targets = jnp.concatenate([user_items[:, 1:], nxt[:1, :1]], axis=1)]
where the time goes in v2:
time: 105 us
  Pallas kernels  102 us (97%)
  local copies, waits for them, and re-layouts  1.94 us (2%)
    pallas_call x1, Pallas kernels, local(): pl.pallas_call(whole_kernel, out_shape=(vm(4, HV, dtype=F32), vm(512, HV)...  102 us

profile of v2, /device:TPU:1, one launch (start us, length us, event | category | flops | bytes accessed | tf_op | source)
XLA Modules:
  0.0 104.5 jit_solution(7111254129350897204)
XLA Ops:
  0.6 101.9 %whole.1 = (f32[4,2048]{1,0:T(4,128)S(1)}, bf16[512,2048]{1,0:T(8,128)(2,1)S(1)}) custom-call(s32[4]{0:T(128)} %lengths.1, bf16[4,256,1024]{2,1,0:T(8,128)(2,1)} %states_h.1, f32[4,16,256]{2,1,0:T(8,128)} %scores_h.1, f32[1,1024]{1,0:T(1,128)} %bitcast.3, bf16[1024,2048]{1,0:T(8,128)(2,1)} %vweight_h.1, bf16[256,2048]{1,0:T(8,128)(2,1)} %pos_h.1, ...), custom_call_target="tpu_custom_call" | custom-call | tf_op jit(solution)/shard_map/whole/pallas_call | solution.py:440
  102.6 0.6 copy.14
  103.2 1.3 %copy.15 = bf16[512,2048]{1,0:T(8,128)(2,1)} copy(bf16[512,2048]{1,0:T(8,128)(2,1)S(1)} %get-tuple-element.3) | data formatting | bytes 4194304

commit v3 on v2

--- a/solution.py
+++ b/solution.py
@@ -12,7 +12,7 @@
 TILES, CHUNK = 4, 512
 VM = pl.BlockSpec(memory_space=pltpu.VMEM)
 ANY = pl.BlockSpec(memory_space=pl.ANY)
-COPIES = 208
+COPIES = 250
 
 
 def place():
@@ -49,16 +49,16 @@
     return hi, (v - hi.astype(F32)).astype(BF16)
 
 
-def meet(peers):
+def greet(peers):
     barrier = pltpu.get_barrier_semaphore()
     for x, y, z, c in peers:
         pl.semaphore_signal(barrier, inc=1, device_id=((x * NZ + z) * 2 + c, y), device_id_type=MESH)
-    pl.semaphore_wait(barrier, len(peers))
+    return barrier, len(peers)
 
 
 class Net:
     def __init__(self, send, recv):
-        self.send, self.recv, self.all = send, recv, []
+        self.send, self.recv, self.all, self.sent = send, recv, [], 0
 
     def put(self, src, dst, where):
         x, y, z, c = where
@@ -76,9 +76,11 @@
         self.all.append(copy)
         return copy
 
-    def drain(self):
-        for copy in self.all:
+    def drain(self, upto=None):
+        upto = len(self.all) if upto is None else upto
+        for copy in self.all[self.sent:upto]:
             copy.wait_send()
+        self.sent = upto
 
 
 def landed(copies):
@@ -94,13 +96,13 @@
 
 
 def whole_kernel(
-    lengths, states_h, scores_h, igain, vweight_h, pos_h, ugain, uweight_h, ids, negs,
+    lengths_h, states_h, scores_h, igain_h, vweight_h, pos_h, ugain_h, uweight_h, ids_h, negs_h,
     item_out, weight_out,
-    states, scores, vweight, uweight, pos, ids8,
+    lengths, igain, ugain, ids, negs, states, scores, vweight, uweight, pos, ids8,
     squares, squares_in, num, num_in, cat, ep, ep_in, pin, pback, pback_in, posx, nxt, ce, pp,
     in_v, ep_v, u_v, uh_v, ug_v, iu_v,
     s, q, r, s1_in, q1_in, r1_in, s1, q1, r1, s2_in, r2_in, q2_in, s2, r2, q2, s3_in, r3_in, q3_in, s3, s4_in,
-    qg, sg, t, t_in, item,
+    qg, sg, t, t_in, t2, t2_in, item,
     send, recv, local,
 ):
     x, y, z, c = place()
@@ -128,23 +130,28 @@
         pltpu.make_async_copy(vweight_h, vweight, local.at[4]),
         pltpu.make_async_copy(pos_h.at[:, pl.ds(at128(512 * y + 128 * x), 128)], posx.at[y], local.at[5]),
         pltpu.make_async_copy(pos_h, pos, local.at[6]),
+        pltpu.make_async_copy(lengths_h, lengths, local.at[7]),
+        pltpu.make_async_copy(igain_h, igain, local.at[8]),
+        pltpu.make_async_copy(ugain_h, ugain, local.at[9]),
+        pltpu.make_async_copy(ids_h, ids, local.at[10]),
+        pltpu.make_async_copy(negs_h, negs, local.at[11]),
     ]
-    for load in loads:
-        load.start()
-    ids8[...] = jnp.broadcast_to(ids[...], (8, 256))
+    loads[0].start()
     offsets = [(om, oy) for om in range(4) for oy in range(4) if om or oy]
     zs, xs, ys = range(1, NZ), range(1, NX), range(1, NY)
-    zc = [(dz, dc) for dc in range(2) for dz in range(NZ) if dz or dc]
     xy = [(dx, dy) for dx in range(NX) for dy in range(NY) if dx or dy]
-    meet(
+    barrier, count = greet(
         [mate(om, oy) for om, oy in offsets]
-        + [peer(dz=dz, dc=dc) for dz, dc in zc]
-        + [peer(dx=dx, dy=dy) for dx, dy in xy]
+        + [peer(dz=o) for o in zs]
+        + [peer(dx=dx, dy=dy) for dx, dy in xy if dx]
     )
-
-    pin_copies = [
-        net.put(pos_h.at[rows16, pl.ds(at128(512 * ring(y, o, NY)), 512)], pin.at[o], peer(dy=o)) for o in ys
-    ]
+    for load in loads[7:]:
+        load.start()
+    for load in loads[1:7]:
+        load.start()
+    for load in loads[7:]:
+        load.wait()
+    ids8[...] = jnp.broadcast_to(ids[...], (8, 256))
 
     loads[0].wait()
     ones = jnp.ones((8, 128), BF16)
@@ -159,7 +166,17 @@
         rest = (part - hi.astype(F32) - lo.astype(F32)).astype(BF16)
         sums = jnp.where(item_row == i, nt(ones, hi) + nt(ones, lo) + nt(ones, rest), sums)
     squares[...] = sums
+    pl.semaphore_wait(barrier, count)
     square_copies = [net.put(squares, squares_in.at[o - 1], peer(dy=o)) for o in ys]
+    pin_copies = [
+        net.put(pos_h.at[rows16, pl.ds(at128(512 * ring(y, o, NY)), 512)], pin.at[o], peer(dy=o)) for o in ys
+    ]
+    next_copy = net.put(ids8, nxt, peer(dy=-1))
+    loads[3].wait()
+    token = lax.broadcasted_iota(jnp.int32, (16, 256), 1)
+    for i in range(4):
+        weights = jnp.where(token < lengths[i], jnp.exp(scores[i]), 0.0)
+        scores[i] = weights / jnp.sum(weights, axis=1, keepdims=True)
 
     loads[1].wait()
     loads[2].wait()
@@ -171,15 +188,11 @@
     ).reshape(4, 16, 512)
     back_copies = [net.put(pback.at[o], pback_in.at[o - 1], peer(dy=-o)) for o in ys]
 
-    loads[3].wait()
     landed(square_copies)
     inv_rms = lax.rsqrt((squares[...] + squares_in[0] + squares_in[1] + squares_in[2]) / D + 1e-05)
-    token = lax.broadcasted_iota(jnp.int32, (16, 256), 1)
     pooled_hi, pooled_lo = [], []
     for i in range(4):
-        weights = jnp.where(token < lengths[i], jnp.exp(scores[i]), 0.0)
-        weights = weights * (inv_rms[i:i + 1] / jnp.sum(weights, axis=1, keepdims=True))
-        hi, lo = split(weights)
+        hi, lo = split(scores[i] * inv_rms[i:i + 1])
         both = mm(jnp.concatenate([hi, lo], axis=0), states[i])
         pooled = (both[:16] + both[16:]) * igain[...]
         hi, lo = split(pooled)
@@ -198,6 +211,7 @@
     for om, oy in offsets:
         num_copies.append(net.put(num.at[ring(y, oy, NY)], num_in.at[oy, member], mate(om, oy)))
     num_in[0, pl.ds(member, 1)] = num[pl.ds(y, 1)]
+    mark = len(net.all) - 15
 
     landed(back_copies)
     pp[pl.ds(quarter, 1), rows16] = (pback[0] + pback_in[0] + pback_in[1] + pback_in[2]).astype(BF16)[None]
@@ -223,43 +237,62 @@
     own = pp.at[pl.ds(2 * c, 2), rows64]
     pp_x = [net.put(own, own, peer(dx=o)) for o in xs]
 
+    net.drain(mark)
+    mark = len(net.all) - 17
     landed(ep_copies)
     ce[1, pl.ds(y, 1), rows16, part] = (ep[pl.ds(y, 1)] + ep_in[0] + ep_in[1] + ep_in[2]).astype(BF16)
     block = ce.at[1, y, rows16, part]
     ep_z = [net.put(block, block, peer(dz=o)) for o in zs]
 
+    halves = [pl.ds(at128(256 * c + 128 * h), 128) for h in range(2)]
+
+    def second(a):
+        by_x = [net.put(ce.at[a, y, rows64, halves[0]], ce.at[a, y, rows64, halves[0]], peer(dx=o)) for o in xs]
+        by_y = [net.put(ce.at[a, y, rows64, halves[1]], ce.at[a, y, rows64, halves[1]], peer(dy=o)) for o in ys]
+        return by_x, by_y
+
+    def third(a, by_x, by_y):
+        landed(by_x)
+        block = ce.at[a, y, :, halves[0]]
+        to_y = [net.put(block, block, peer(dy=o)) for o in ys]
+        landed(by_y)
+        block = ce.at[a, :, rows64, halves[1]]
+        to_x = [net.put(block, block, peer(dx=o)) for o in xs]
+        block = ce.at[a, y, :, halves[0]]
+        shared = [net.put(block, block, peer(dc=1))]
+        block = ce.at[a, :, rows64, halves[1]]
+        shared.append(net.put(block, block, peer(dc=1)))
+        return to_y, to_x, shared
+
+    def fourth(a, to_y, to_x, shared):
+        for o in range(1, 4):
+            to_y[o - 1].wait_recv()
+            block = ce.at[a, ring(y, -o, NY), :, halves[0]]
+            shared.append(net.put(block, block, peer(dc=1)))
+            to_x[o - 1].wait_recv()
+            block = ce.at[a, :, pl.ds(at16(64 * ring(x, -o, NX)), 64), halves[1]]
+            shared.append(net.put(block, block, peer(dc=1)))
+        return shared
+
+    net.drain(mark)
+    mark = len(net.all)
     landed(cat_z)
-    block = ce.at[0, y, rows64, mine]
-    cat_x = [net.put(block, block, peer(dx=o)) for o in xs]
+    cat_2 = second(0)
     landed(ep_z)
-    block = ce.at[1, y, rows64, mine]
-    ep_y = [net.put(block, block, peer(dy=o)) for o in ys]
-
+    ep_2 = second(1)
     landed(pp_x)
     own = pp.at[pl.ds(2 * c, 2)]
-    final = [net.put(own, own, peer(dc=1))]
-
-    landed(cat_x)
-    block = ce.at[0, y, :, mine]
-    cat_y = [net.put(block, block, peer(dy=o)) for o in ys]
-    final.append(net.put(block, block, peer(dc=1)))
-    landed(ep_y)
-    block = ce.at[1, :, rows64, mine]
-    ep_x = [net.put(block, block, peer(dx=o)) for o in xs]
-    final.append(net.put(block, block, peer(dc=1)))
-    for o in ys:
-        cat_y[o - 1].wait_recv()
-        block = ce.at[0, ring(y, -o, NY), :, mine]
-        final.append(net.put(block, block, peer(dc=1)))
-    for o in xs:
-        ep_x[o - 1].wait_recv()
-        block = ce.at[1, :, pl.ds(at16(64 * ring(x, -o, NX)), 64), mine]
-        final.append(net.put(block, block, peer(dc=1)))
-    next_copy = net.put(ids8, nxt, peer(dy=-1))
+    pp_final = net.put(own, own, peer(dc=1))
+    cat_3 = third(0, *cat_2)
+    ep_3 = third(1, *ep_2)
+    cat_4 = fourth(0, *cat_3)
+    ep_4 = fourth(1, *ep_3)
     posx_copies = [
         net.put(pos_h.at[:, pl.ds(at128(512 * ring(y, o, NY) + 128 * x), 128)], posx.at[y], peer(dy=o)) for o in ys
     ]
-    landed(final)
+    net.drain(mark)
+    mark = len(net.all)
+    landed(cat_4)
     landed([next_copy])
     loads[6].wait()
 
@@ -285,6 +318,8 @@
         cat_squares += jnp.sum(w * w, axis=1, keepdims=True)
     inv = lax.rsqrt(in_squares / HV + 1e-05)
     cat_inv = 1.0 / jnp.sqrt(cat_squares + 1e-06)
+    landed(ep_4)
+    pp_final.wait_recv()
     out_squares = jnp.zeros((256, 1), F32)
     for k, j in enumerate(js):
         e = mm(hot, ce[1, k]) + pp[k].astype(F32)
@@ -304,48 +339,60 @@
     pos_power = jnp.sum(target_t * powers, axis=0, keepdims=True)
     total = pos_power + jnp.sum(counts * powers, axis=0, keepdims=True)
     grad_t = scale * (counts * powers / total + target_t * (pos_power / total - 1.0))
-    by_item = grad_t.astype(BF16)
     by_row_hi, by_row_lo = split((grad_t * cat_inv).T)
     along = jnp.zeros((256, 1), F32)
-    cat_along = jnp.zeros((256, 1), F32)
     for k, j in enumerate(js):
         v = 20.0 * (mm(by_row_hi, ce[0, k]) + mm(by_row_lo, ce[0, k]))
         ug_v[:, j] = v
         along += jnp.sum(v * u_v[:, j], axis=1, keepdims=True)
-        v = 20.0 * mm(by_item, uh_v[:, j])
-        iu_v[:, j] = v
-        cat_along += jnp.sum(v * ce[0, k].astype(F32), axis=1, keepdims=True)
-    cat_along = cat_along * cat_inv * cat_inv
     inner = jnp.zeros((256, 1), F32)
-    for j in js:
+    s1_copies, q1_copies, r1_copies, s2_copies, q2_copies = [], [], [], [], []
+
+    def chips(k):
+        q1_copies[k].wait_recv()
+        q1[k] = (q[k, :, mine].astype(F32) + q1_in[k].astype(F32)).astype(BF16)
+        for o in xs:
+            rows = pl.ds(at16(64 * ring(x, o, NX)), 64)
+            q2_copies.append(net.put(q1.at[k, rows], q2_in.at[o - 1, k], peer(dx=o)))
+        s1_copies[k].wait_recv()
+        s1[k] = (s[k, :, mine].astype(F32) + s1_in[k].astype(F32)).astype(BF16)
+        for o in ys:
+            rows = pl.ds(at16(64 * ring(y, o, NY)), 64)
+            s2_copies.append(net.put(s1.at[k, rows], s2_in.at[o - 1, k], peer(dy=o)))
+
+    for k, j in enumerate(js):
         g = (ug_v[:, j] - u_v[:, j] * along) * out_inv
         ug_v[:, j] = g
-        inner += jnp.sum(g * ep_v[:, j], axis=1, keepdims=True)
-    inner = inner * (inv * inv * inv / HV)
-    s1_copies, q1_copies, r1_copies = [], [], []
-    for k, j in enumerate(js):
-        g = ug_v[:, j]
         rows = (inv * g).astype(BF16)
         q[k] = rows
         q1_copies.append(net.put(q.at[k, :, theirs], q1_in.at[k], peer(dc=1)))
         s[k] = mm(hot_t, rows).astype(BF16)
         s1_copies.append(net.put(s.at[k, :, theirs], s1_in.at[k], peer(dc=1)))
-        direct = (g - in_v[:, j] * inner).astype(BF16)
+        inner += jnp.sum(g * ep_v[:, j], axis=1, keepdims=True)
+        if k:
+            chips(k - 1)
+    inner = inner * (inv * inv * inv / HV)
+    by_item = grad_t.astype(BF16)
+    cat_along = jnp.zeros((256, 1), F32)
+    for k, j in enumerate(js):
+        v = 20.0 * mm(by_item, uh_v[:, j])
+        iu_v[:, j] = v
+        cat_along += jnp.sum(v * ce[0, k].astype(F32), axis=1, keepdims=True)
+        if k == 0:
+            chips(TILES - 1)
+    cat_along = cat_along * cat_inv * cat_inv
+    for k, j in enumerate(js):
+        direct = (ug_v[:, j] - in_v[:, j] * inner).astype(BF16)
         item_grad = (iu_v[:, j] - ce[0, k].astype(F32) * cat_along) * cat_inv
         r[k] = (mm(hot_t, direct) + item_grad).astype(BF16)
         r1_copies.append(net.put(r.at[k, :, theirs], r1_in.at[k], peer(dc=1)))
-
     for k in range(TILES):
-        q1_copies[k].wait_recv()
-        q1[k] = (q[k, :, mine].astype(F32) + q1_in[k].astype(F32)).astype(BF16)
-        s1_copies[k].wait_recv()
-        s1[k] = (s[k, :, mine].astype(F32) + s1_in[k].astype(F32)).astype(BF16)
         r1_copies[k].wait_recv()
         r1[k] = (r[k, :, mine].astype(F32) + r1_in[k].astype(F32)).astype(BF16)
-    s2_copies = [net.put(s1.at[:, pl.ds(at16(64 * ring(y, o, NY)), 64)], s2_in.at[o - 1], peer(dy=o)) for o in ys]
-    q2_copies = [net.put(q1.at[:, pl.ds(at16(64 * ring(x, o, NX)), 64)], q2_in.at[o - 1], peer(dx=o)) for o in xs]
     r2_copies = [net.put(r1.at[ring(y, o, NY)], r2_in.at[o - 1], peer(dy=o)) for o in ys]
 
+    net.drain(mark)
+    mark = len(net.all)
     landed(s2_copies)
     s2[...] = added(s1[:, pl.ds(at16(64 * y), 64)], s2_in, 3).astype(BF16)
     s3_copies = [net.put(s2.at[:, pl.ds(at16(16 * ring(x, o, NX)), 16)], s3_in.at[o - 1], peer(dx=o)) for o in xs]
@@ -359,15 +406,15 @@
     for o in zs:
         k, part = slot(ring(z, o, NZ))
         q3_copies.append(net.put(q2.at[k, :, part], q3_in.at[o - 1], peer(dz=o)))
-    landed(r2_copies)
-    r2[...] = added(r1[pl.ds(y, 1)][0], r2_in, 3).astype(BF16)
-    r3_copies = [net.put(r2.at[pl.ds(at16(64 * ring(x, o, NX)), 64)], r3_in.at[o - 1], peer(dx=o)) for o in xs]
     landed(s3_copies)
     s3[...] = added(s2[:, pl.ds(at16(16 * x), 16)], s3_in, 3).astype(BF16)
     s4_copies = []
     for o in zs:
         k, part = slot(ring(z, o, NZ))
         s4_copies.append(net.put(s3.at[k, :, part], s4_in.at[o - 1], peer(dz=o)))
+    landed(r2_copies)
+    r2[...] = added(r1[pl.ds(y, 1)][0], r2_in, 3).astype(BF16)
+    r3_copies = [net.put(r2.at[pl.ds(at16(64 * ring(x, o, NX)), 64)], r3_in.at[o - 1], peer(dx=o)) for o in xs]
     spot = 4 * y + x
     own, part = slot(z)
     landed(q3_copies)
@@ -376,52 +423,60 @@
     landed(s4_copies)
     sg[pl.ds(spot, 1)] = added(s3[pl.ds(own, 1), :, part][0], s4_in, NZ - 1).astype(BF16)[None]
     sg_copies = [net.put(sg.at[spot], sg.at[spot], peer(dx=dx, dy=dy)) for dx, dy in xy]
-    landed(r3_copies)
-    r3 = added(r2[rows64], r3_in, 3)
 
     gain_rows = ugain[:, pl.ds(at128(512 * y + 128 * x), 128)]
     loads[5].wait()
     landed(posx_copies)
     positions = (posx[...].astype(F32).reshape(1024, 128) * gain_rows).astype(BF16)
     embeds = (ce[0, pl.ds(y, 1), :, pl.ds(at128(128 * x), 128)][0].astype(F32) * gain_rows).astype(BF16)
+    net.drain(mark)
+    mark = len(net.all)
     landed(qg_copies)
     tile = tn(positions, qg[...].reshape(1024, 128))
     landed(sg_copies)
     tile = tile + tn(embeds, sg[...].reshape(256, 128))
     wrows = pl.ds(at16(128 * x), 128)
-    zcols = pl.ds(at128(512 * lax.div(z, 2) + 256 * c + 128 * low), 128)
-    weight_out[wrows, zcols] = tile.astype(BF16)
-    block = weight_out.at[wrows, zcols]
-    weight_z = [net.put(block, block, peer(dz=o)) for o in zs]
-
-    back = nt(sg[pl.ds(4 * x, 4)].reshape(64, 128), uweight[:, zcols]) * gain_part
+
+    def zcols(i):
+        return pl.ds(at128(512 * lax.div(i, 2) + 256 * c + 128 * lax.rem(i, 2)), 128)
+
+    weight_out[wrows, zcols(z)] = tile.astype(BF16)
+    block = weight_out.at[wrows, zcols(z)]
+    near = [1, 7, 2, 6, 3, 5, 4]
+    weight_z = [net.put(block, block, peer(dz=o)) for o in near]
+    weight_x = [[net.put(block, block, peer(dx=o)) for o in xs]]
+
+    back = nt(sg[pl.ds(4 * x, 4)].reshape(64, 128), uweight[:, zcols(z)]) * gain_part
     half = lax.broadcasted_iota(jnp.int32, (64, 512), 1) // 256
+    landed(r3_copies)
+    r3 = added(r2[rows64], r3_in, 3)
     back = back + jnp.where(half == c, jnp.concatenate([r3, r3], axis=1), 0.0)
     back = back.reshape(16, 4, 512)
-    t[...] = jnp.concatenate([back[:, :, :256], back[:, :, 256:]], axis=1)
-    t_copies = []
-    for k, (dz, dc) in enumerate(zc):
-        to = peer(dz=dz, dc=dc)
-        t_copies.append(net.put(t.at[2 * to[2] + to[3]], t_in.at[k], to))
-
-    landed(weight_z)
-    weight_x, final = [], []
-    for k in range(TILES):
-        block = weight_out.at[wrows, pl.ds(at128(512 * k + 256 * c), 256)]
+    t[...] = jnp.concatenate([back[:, :, :256], back[:, :, 256:]], axis=1).reshape(8, 2, 8, 256)
+    t_copies = [net.put(t.at[ring(z, o, NZ)], t_in.at[o - 1], peer(dz=o)) for o in zs]
+
+    for o, copy in zip(near, weight_z):
+        copy.wait_recv()
+        block = weight_out.at[wrows, zcols(ring(z, -o, NZ))]
         weight_x.append([net.put(block, block, peer(dx=o)) for o in xs])
+    landed(t_copies)
+    t2[...] = added(t[pl.ds(z, 1)][0], t_in, NZ - 1)
+    t2_copy = net.put(t2.at[ring(c, 1, 2)], t2_in, peer(dc=1))
+    final = []
+    for o, copies in zip([0] + near[:3], weight_x[:4]):
+        landed(copies)
+        block = weight_out.at[:, zcols(ring(z, -o, NZ))]
         final.append(net.put(block, block, peer(dc=1)))
-
-    landed(t_copies)
-    total = added(t[pl.ds(2 * z + c, 1)][0], t_in, len(zc))
-    item[pl.ds(y, 1)] = total[None]
+    net.drain(mark)
+    mark = len(net.all) - 4
+    t2_copy.wait_recv()
+    item[pl.ds(y, 1)] = t2[pl.ds(c, 1)] + t2_in[...][None]
     item_copies = [net.put(item.at[y], item.at[y], peer(dy=o)) for o in ys]
-
-    for k in range(TILES):
-        for o in xs:
-            weight_x[k][o - 1].wait_recv()
-            rows = pl.ds(at16(128 * ring(x, -o, NX)), 128)
-            block = weight_out.at[rows, pl.ds(at128(512 * k + 256 * c), 256)]
-            final.append(net.put(block, block, peer(dc=1)))
+    for o, copies in zip(near[3:], weight_x[4:]):
+        landed(copies)
+        block = weight_out.at[:, zcols(ring(z, -o, NZ))]
+        final.append(net.put(block, block, peer(dc=1)))
+    net.drain(mark)
     landed(item_copies)
     for k in range(NY):
         item_out[:, 512 * k:512 * k + 256] = item[k, :4]
@@ -440,9 +495,11 @@
     return pl.pallas_call(
         whole_kernel,
         out_shape=(vm(4, HV, dtype=F32), vm(512, HV)),
-        in_specs=[pl.BlockSpec(memory_space=pltpu.SMEM), ANY, ANY, VM, ANY, ANY, VM, ANY, VM, VM],
+        in_specs=[ANY] * 10,
         out_specs=(VM, VM),
         scratch_shapes=[
+            pltpu.SMEM((4,), jnp.int32), vm(1, 1024, dtype=F32), vm(1, HV, dtype=F32),
+            vm(1, 256, dtype=jnp.int32), vm(1, 256, dtype=jnp.int32),
             vm(4, 256, 1024), vm(4, 16, 256, dtype=F32), vm(1024, HV), vm(512, HV), vm(256, HV),
             vm(8, 256, dtype=jnp.int32),
             vm(8, 256, dtype=F32), vm(3, 8, 256, dtype=F32),
@@ -461,10 +518,11 @@
             vm(3, 4, 16, 256), vm(3, 64, 256), vm(7, 64, 128),
             vm(4, 16, 256), vm(7, 16, 128),
             vm(16, 64, 128), vm(16, 16, 128),
-            vm(16, 8, 256, dtype=F32), vm(15, 8, 256, dtype=F32), vm(4, 8, 256, dtype=F32),
+            vm(8, 2, 8, 256, dtype=F32), vm(7, 2, 8, 256, dtype=F32), vm(2, 8, 256, dtype=F32),
+            vm(8, 256, dtype=F32), vm(4, 8, 256, dtype=F32),
             pltpu.SemaphoreType.DMA((COPIES,)),
             pltpu.SemaphoreType.DMA((COPIES,)),
-            pltpu.SemaphoreType.DMA((7,)),
+            pltpu.SemaphoreType.DMA((12,)),
         ],
         compiler_params=pltpu.CompilerParams(
             collective_id=0, has_side_effects=True, vmem_limit_bytes=60 * 2**20

time: 105 us -> 90.2 us (0.86)
  Pallas kernels: 102 us -> 87.6 us
    pallas_call x1, Pallas kernels: 102 us -> 87.6 us  [local(): pl.pallas_call(whole_kernel, out_shape=(vm(4, HV, dtype=F32), vm(512, HV)...]
where the time goes in v3:
time: 90.2 us; the launch traced here: 90.1 us
  Pallas kernels  87.6 us (97%)
  local copies, waits for them, and re-layouts  1.94 us (2%)
    pallas_call x1, Pallas kernels, local(): pl.pallas_call(whole_kernel, out_shape=(vm(4, HV, dtype=F32), vm(512, HV)...  87.6 us
    unnamed x2, local copies, waits for them, and re-layouts  1.94 us

profile of v3, /device:TPU:1, one launch (start us, length us, event | category | flops | bytes accessed | tf_op | source)
XLA Modules:
  0.0 90.1 jit_solution(17772512505037958043)
XLA Ops:
  0.6 87.6 %whole.1 = (f32[4,2048]{1,0:T(4,128)S(1)}, bf16[512,2048]{1,0:T(8,128)(2,1)S(1)}) custom-call(s32[4]{0:T(128)} %lengths_h.1, bf16[4,256,1024]{2,1,0:T(8,128)(2,1)} %states_h.1, f32[4,16,256]{2,1,0:T(8,128)} %scores_h.1, f32[1,1024]{1,0:T(1,128)} %bitcast.3, bf16[1024,2048]{1,0:T(8,128)(2,1)} %vweight_h.1, bf16[256,2048]{1,0:T(8,128)(2,1)} %pos_h.1, ...), custom_call_target="tpu_custom_call" | custom-call | tf_op jit(solution)/shard_map/whole/pallas_call | solution.py:495
  88.2 0.6 copy.14
  88.8 1.3 %copy.15 = bf16[512,2048]{1,0:T(8,128)(2,1)} copy(bf16[512,2048]{1,0:T(8,128)(2,1)S(1)} %get-tuple-element.3) | data formatting | bytes 4194304

commit v4 on v3

--- a/solution.py
+++ b/solution.py
@@ -20,8 +20,23 @@
     return lax.div(d, 16), y, lax.rem(lax.div(d, 2), 8), lax.rem(d, 2)
 
 
-def ring(i, o, n):
-    return lax.rem(i + o + n, n)
+class Indices:
+    def __init__(self):
+        self.known = {}
+
+    def ring(self, i, o, n):
+        key = (id(i), o % n, n)
+        if key not in self.known:
+            ahead = i + o % n
+            self.known[key] = (i, jnp.where(ahead >= n, ahead - n, ahead) if o % n else i)
+        return self.known[key][1]
+
+    def halves(self, i):
+        key = (id(i), 2)
+        if key not in self.known:
+            half = sum(jnp.where(i >= k, 1, 0) for k in (2, 4, 6))
+            self.known[key] = (i, (half, i - 2 * half))
+        return self.known[key][1]
 
 
 def at128(i):
@@ -100,14 +115,16 @@
     item_out, weight_out,
     lengths, igain, ugain, ids, negs, states, scores, vweight, uweight, pos, ids8,
     squares, squares_in, num, num_in, cat, ep, ep_in, pin, pback, pback_in, posx, nxt, ce, pp,
-    in_v, ep_v, u_v, uh_v, ug_v, iu_v,
+    in_v, ep_v, u_v, uh_v, ug_v,
     s, q, r, s1_in, q1_in, r1_in, s1, q1, r1, s2_in, r2_in, q2_in, s2, r2, q2, s3_in, r3_in, q3_in, s3, s4_in,
     qg, sg, t, t_in, t2, t2_in, item,
     send, recv, local,
 ):
     x, y, z, c = place()
-    low = lax.rem(z, 2)
-    group = 4 * x + lax.div(z, 2)
+    indices = Indices()
+    ring, halves_of = indices.ring, indices.halves
+    pair, low = halves_of(z)
+    group = 4 * x + pair
     member, quarter = 2 * low + c, 2 * c + low
     base = z - low
     net = Net(send, recv)
@@ -117,54 +134,55 @@
 
     def mate(om, oy):
         m = ring(member, om, 4)
-        return x, ring(y, oy, NY), base + lax.div(m, 2), lax.rem(m, 2)
+        hi, lo = halves_of(m)
+        return x, ring(y, oy, NY), base + hi, lo
 
     rows16, rows64 = pl.ds(at16(16 * group), 16), pl.ds(at16(64 * x), 64)
     mine, theirs = pl.ds(at128(256 * c), 256), pl.ds(at128(256 * ring(c, 1, 2)), 256)
     own512 = pl.ds(at128(512 * y), 512)
     loads = [
-        pltpu.make_async_copy(states_h, states, local.at[0]),
-        pltpu.make_async_copy(pos_h.at[rows16, own512], pin.at[0], local.at[1]),
-        pltpu.make_async_copy(uweight_h, uweight, local.at[2]),
-        pltpu.make_async_copy(scores_h, scores, local.at[3]),
-        pltpu.make_async_copy(vweight_h, vweight, local.at[4]),
-        pltpu.make_async_copy(pos_h.at[:, pl.ds(at128(512 * y + 128 * x), 128)], posx.at[y], local.at[5]),
-        pltpu.make_async_copy(pos_h, pos, local.at[6]),
+        pltpu.make_async_copy(pos_h.at[rows16, own512], pin.at[0], local.at[0]),
+        pltpu.make_async_copy(uweight_h, uweight, local.at[1]),
+        pltpu.make_async_copy(scores_h, scores, local.at[2]),
+        pltpu.make_async_copy(vweight_h, vweight, local.at[3]),
+        pltpu.make_async_copy(pos_h.at[:, pl.ds(at128(512 * y + 128 * x), 128)], posx.at[y], local.at[4]),
+        pltpu.make_async_copy(pos_h, pos, local.at[5]),
         pltpu.make_async_copy(lengths_h, lengths, local.at[7]),
         pltpu.make_async_copy(igain_h, igain, local.at[8]),
         pltpu.make_async_copy(ugain_h, ugain, local.at[9]),
         pltpu.make_async_copy(ids_h, ids, local.at[10]),
         pltpu.make_async_copy(negs_h, negs, local.at[11]),
     ]
-    loads[0].start()
+    item_loads = [pltpu.make_async_copy(states_h.at[i], states.at[i], local.at[12 + i]) for i in range(4)]
+    for load in item_loads:
+        load.start()
+    loads[2].start()
     offsets = [(om, oy) for om in range(4) for oy in range(4) if om or oy]
-    zs, xs, ys = range(1, NZ), range(1, NX), range(1, NY)
+    zs, xs, ys = (4, 3, 5, 2, 6, 1, 7), range(1, NX), range(1, NY)
     xy = [(dx, dy) for dx in range(NX) for dy in range(NY) if dx or dy]
     barrier, count = greet(
         [mate(om, oy) for om, oy in offsets]
         + [peer(dz=o) for o in zs]
         + [peer(dx=dx, dy=dy) for dx, dy in xy if dx]
     )
-    for load in loads[7:]:
+    for load in loads[6:]:
         load.start()
-    for load in loads[1:7]:
-        load.start()
-    for load in loads[7:]:
-        load.wait()
-    ids8[...] = jnp.broadcast_to(ids[...], (8, 256))
-
-    loads[0].wait()
-    ones = jnp.ones((8, 128), BF16)
+
+    ones = jnp.ones((8, 256), BF16)
     item_row = lax.broadcasted_iota(jnp.int32, (8, 256), 0)
     sums = jnp.zeros((8, 256), F32)
     for i in range(4):
+        item_loads[i].wait()
         part = jnp.zeros((256, 128), F32)
         for j in range(8):
             v = states[i, :, 128 * j:128 * (j + 1)].astype(F32)
             part = part + v * v
-        hi, lo = split(part)
-        rest = (part - hi.astype(F32) - lo.astype(F32)).astype(BF16)
-        sums = jnp.where(item_row == i, nt(ones, hi) + nt(ones, lo) + nt(ones, rest), sums)
+        sums = jnp.where(item_row == i, nt(ones, jnp.concatenate(split(part), axis=1)), sums)
+    for k in (0, 1, 3, 5, 4):
+        loads[k].start()
+    for load in loads[6:]:
+        load.wait()
+    ids8[...] = jnp.broadcast_to(ids[...], (8, 256))
     squares[...] = sums
     pl.semaphore_wait(barrier, count)
     square_copies = [net.put(squares, squares_in.at[o - 1], peer(dy=o)) for o in ys]
@@ -172,14 +190,14 @@
         net.put(pos_h.at[rows16, pl.ds(at128(512 * ring(y, o, NY)), 512)], pin.at[o], peer(dy=o)) for o in ys
     ]
     next_copy = net.put(ids8, nxt, peer(dy=-1))
-    loads[3].wait()
+    loads[2].wait()
     token = lax.broadcasted_iota(jnp.int32, (16, 256), 1)
     for i in range(4):
         weights = jnp.where(token < lengths[i], jnp.exp(scores[i]), 0.0)
         scores[i] = weights / jnp.sum(weights, axis=1, keepdims=True)
 
+    loads[0].wait()
     loads[1].wait()
-    loads[2].wait()
     landed(pin_copies)
     gain_part = ugain[:, own512]
     pos_rows = pin[...].astype(F32).reshape(64, 512) * gain_part
@@ -199,7 +217,7 @@
         pooled_hi.append(hi)
         pooled_lo.append(lo)
     left = jnp.concatenate(pooled_hi + pooled_lo, axis=0)
-    loads[4].wait()
+    loads[3].wait()
     head = lax.broadcasted_iota(jnp.int32, (4, 16, 256), 1)
     tile = lax.broadcasted_iota(jnp.int32, (4, 16, 256), 2) // 128
     for j in range(8):
@@ -294,7 +312,7 @@
     mark = len(net.all)
     landed(cat_4)
     landed([next_copy])
-    loads[6].wait()
+    loads[5].wait()
 
     js = [slice(CHUNK * k, CHUNK * (k + 1)) for k in range(TILES)]
     all_items = lax.broadcasted_iota(jnp.int32, (256, 256), 0)
@@ -330,38 +348,36 @@
     out_inv = 1.0 / jnp.sqrt(out_squares + 1e-06)
     logits = jnp.zeros((256, 256), F32)
     for k, j in enumerate(js):
-        u = u_v[:, j] * out_inv
-        u_v[:, j] = u
-        hi, lo = split(u)
+        hi, lo = split(u_v[:, j] * out_inv)
         uh_v[:, j] = hi
         logits += nt(ce[0, k], hi) + nt(ce[0, k], lo)
-    powers = jnp.exp(20.0 * cat_inv * logits)
+    logits = 20.0 * cat_inv * logits
+    powers = jnp.exp(logits)
     pos_power = jnp.sum(target_t * powers, axis=0, keepdims=True)
     total = pos_power + jnp.sum(counts * powers, axis=0, keepdims=True)
     grad_t = scale * (counts * powers / total + target_t * (pos_power / total - 1.0))
-    by_row_hi, by_row_lo = split((grad_t * cat_inv).T)
-    along = jnp.zeros((256, 1), F32)
-    for k, j in enumerate(js):
-        v = 20.0 * (mm(by_row_hi, ce[0, k]) + mm(by_row_lo, ce[0, k]))
-        ug_v[:, j] = v
-        along += jnp.sum(v * u_v[:, j], axis=1, keepdims=True)
+    moved = grad_t * logits
+    cat_along = jnp.sum(moved, axis=1, keepdims=True) * cat_inv
+    along = jnp.sum(moved.T, axis=1, keepdims=True) * out_inv
+    by_row, by_row_lo = split((grad_t * (20.0 * cat_inv)).T)
     inner = jnp.zeros((256, 1), F32)
     s1_copies, q1_copies, r1_copies, s2_copies, q2_copies = [], [], [], [], []
 
     def chips(k):
         q1_copies[k].wait_recv()
         q1[k] = (q[k, :, mine].astype(F32) + q1_in[k].astype(F32)).astype(BF16)
-        for o in xs:
+        for o in xs if k % 2 else ():
             rows = pl.ds(at16(64 * ring(x, o, NX)), 64)
-            q2_copies.append(net.put(q1.at[k, rows], q2_in.at[o - 1, k], peer(dx=o)))
+            q2_copies.append(net.put(q1.at[k - 1:k + 1, rows], q2_in.at[o - 1, k - 1:k + 1], peer(dx=o)))
         s1_copies[k].wait_recv()
         s1[k] = (s[k, :, mine].astype(F32) + s1_in[k].astype(F32)).astype(BF16)
-        for o in ys:
+        for o in ys if k % 2 else ():
             rows = pl.ds(at16(64 * ring(y, o, NY)), 64)
-            s2_copies.append(net.put(s1.at[k, rows], s2_in.at[o - 1, k], peer(dy=o)))
+            s2_copies.append(net.put(s1.at[k - 1:k + 1, rows], s2_in.at[o - 1, k - 1:k + 1], peer(dy=o)))
 
     for k, j in enumerate(js):
-        g = (ug_v[:, j] - u_v[:, j] * along) * out_inv
+        g = mm(by_row, ce[0, k]) + mm(by_row_lo, ce[0, k])
+        g = (g - u_v[:, j] * along) * out_inv
         ug_v[:, j] = g
         rows = (inv * g).astype(BF16)
         q[k] = rows
@@ -373,17 +389,10 @@
             chips(k - 1)
     inner = inner * (inv * inv * inv / HV)
     by_item = grad_t.astype(BF16)
-    cat_along = jnp.zeros((256, 1), F32)
-    for k, j in enumerate(js):
-        v = 20.0 * mm(by_item, uh_v[:, j])
-        iu_v[:, j] = v
-        cat_along += jnp.sum(v * ce[0, k].astype(F32), axis=1, keepdims=True)
-        if k == 0:
-            chips(TILES - 1)
-    cat_along = cat_along * cat_inv * cat_inv
+    chips(TILES - 1)
     for k, j in enumerate(js):
         direct = (ug_v[:, j] - in_v[:, j] * inner).astype(BF16)
-        item_grad = (iu_v[:, j] - ce[0, k].astype(F32) * cat_along) * cat_inv
+        item_grad = (20.0 * mm(by_item, uh_v[:, j]) - ce[0, k].astype(F32) * cat_along) * cat_inv
         r[k] = (mm(hot_t, direct) + item_grad).astype(BF16)
         r1_copies.append(net.put(r.at[k, :, theirs], r1_in.at[k], peer(dc=1)))
     for k in range(TILES):
@@ -400,7 +409,8 @@
     q2[...] = added(q1[:, rows64], q2_in, 3).astype(BF16)
 
     def slot(to):
-        return lax.div(to, 2), pl.ds(at128(128 * lax.rem(to, 2)), 128)
+        hi, lo = halves_of(to)
+        return hi, pl.ds(at128(128 * lo), 128)
 
     q3_copies = []
     for o in zs:
@@ -412,20 +422,20 @@
     for o in zs:
         k, part = slot(ring(z, o, NZ))
         s4_copies.append(net.put(s3.at[k, :, part], s4_in.at[o - 1], peer(dz=o)))
-    landed(r2_copies)
-    r2[...] = added(r1[pl.ds(y, 1)][0], r2_in, 3).astype(BF16)
-    r3_copies = [net.put(r2.at[pl.ds(at16(64 * ring(x, o, NX)), 64)], r3_in.at[o - 1], peer(dx=o)) for o in xs]
     spot = 4 * y + x
     own, part = slot(z)
     landed(q3_copies)
     qg[pl.ds(spot, 1)] = added(q2[pl.ds(own, 1), :, part][0], q3_in, NZ - 1).astype(BF16)[None]
     qg_copies = [net.put(qg.at[spot], qg.at[spot], peer(dx=dx, dy=dy)) for dx, dy in xy]
+    landed(r2_copies)
+    r2[...] = added(r1[pl.ds(y, 1)][0], r2_in, 3).astype(BF16)
+    r3_copies = [net.put(r2.at[pl.ds(at16(64 * ring(x, o, NX)), 64)], r3_in.at[o - 1], peer(dx=o)) for o in xs]
     landed(s4_copies)
     sg[pl.ds(spot, 1)] = added(s3[pl.ds(own, 1), :, part][0], s4_in, NZ - 1).astype(BF16)[None]
     sg_copies = [net.put(sg.at[spot], sg.at[spot], peer(dx=dx, dy=dy)) for dx, dy in xy]
 
     gain_rows = ugain[:, pl.ds(at128(512 * y + 128 * x), 128)]
-    loads[5].wait()
+    loads[4].wait()
     landed(posx_copies)
     positions = (posx[...].astype(F32).reshape(1024, 128) * gain_rows).astype(BF16)
     embeds = (ce[0, pl.ds(y, 1), :, pl.ds(at128(128 * x), 128)][0].astype(F32) * gain_rows).astype(BF16)
@@ -438,7 +448,8 @@
     wrows = pl.ds(at16(128 * x), 128)
 
     def zcols(i):
-        return pl.ds(at128(512 * lax.div(i, 2) + 256 * c + 128 * lax.rem(i, 2)), 128)
+        hi, lo = halves_of(i)
+        return pl.ds(at128(512 * hi + 256 * c + 128 * lo), 128)
 
     weight_out[wrows, zcols(z)] = tile.astype(BF16)
     block = weight_out.at[wrows, zcols(z)]
@@ -462,16 +473,16 @@
     landed(t_copies)
     t2[...] = added(t[pl.ds(z, 1)][0], t_in, NZ - 1)
     t2_copy = net.put(t2.at[ring(c, 1, 2)], t2_in, peer(dc=1))
+    net.drain(mark)
+    mark = len(net.all)
+    t2_copy.wait_recv()
+    item[pl.ds(y, 1)] = t2[pl.ds(c, 1)] + t2_in[...][None]
+    item_copies = [net.put(item.at[y], item.at[y], peer(dy=o)) for o in ys]
     final = []
     for o, copies in zip([0] + near[:3], weight_x[:4]):
         landed(copies)
         block = weight_out.at[:, zcols(ring(z, -o, NZ))]
         final.append(net.put(block, block, peer(dc=1)))
-    net.drain(mark)
-    mark = len(net.all) - 4
-    t2_copy.wait_recv()
-    item[pl.ds(y, 1)] = t2[pl.ds(c, 1)] + t2_in[...][None]
-    item_copies = [net.put(item.at[y], item.at[y], peer(dy=o)) for o in ys]
     for o, copies in zip(near[3:], weight_x[4:]):
         landed(copies)
         block = weight_out.at[:, zcols(ring(z, -o, NZ))]
@@ -485,6 +496,17 @@
     net.drain()
 
 
+def deliver_kernel(item_grads, weight_grad, item_out, weight_out, sems):
+    copies = [
+        pltpu.make_async_copy(weight_grad, weight_out, sems.at[0]),
+        pltpu.make_async_copy(item_grads, item_out, sems.at[1]),
+    ]
+    for copy in copies:
+        copy.start()
+    for copy in copies:
+        copy.wait()
+
+
 def local(
     item_states, item_scores, item_lengths, item_gain, value_weight,
     user_items, negatives, position_embed, user_gain, user_weight,
@@ -492,7 +514,7 @@
     def vm(*shape, dtype=BF16):
         return pltpu.VMEM(shape, dtype)
 
-    return pl.pallas_call(
+    item_grads, weight_grad = pl.pallas_call(
         whole_kernel,
         out_shape=(vm(4, HV, dtype=F32), vm(512, HV)),
         in_specs=[ANY] * 10,
@@ -509,7 +531,7 @@
             vm(4, 256, 128), vm(8, 256, dtype=jnp.int32),
             vm(2, 4, 256, 512), vm(4, 256, 512),
             vm(256, HV, dtype=F32), vm(256, HV, dtype=F32), vm(256, HV, dtype=F32), vm(256, HV),
-            vm(256, HV, dtype=F32), vm(256, HV, dtype=F32),
+            vm(256, HV, dtype=F32),
             vm(4, 256, 512), vm(4, 256, 512), vm(4, 256, 512),
             vm(4, 256, 256), vm(4, 256, 256), vm(4, 256, 256),
             vm(4, 256, 256), vm(4, 256, 256), vm(4, 256, 256),
@@ -522,7 +544,7 @@
             vm(8, 256, dtype=F32), vm(4, 8, 256, dtype=F32),
             pltpu.SemaphoreType.DMA((COPIES,)),
             pltpu.SemaphoreType.DMA((COPIES,)),
-            pltpu.SemaphoreType.DMA((12,)),
+            pltpu.SemaphoreType.DMA((16,)),
         ],
         compiler_params=pltpu.CompilerParams(
             collective_id=0, has_side_effects=True, vmem_limit_bytes=60 * 2**20
@@ -532,6 +554,18 @@
         item_lengths, item_states, item_scores, item_gain.reshape(1, -1), value_weight,
         position_embed, user_gain.reshape(1, HV), user_weight, user_items, negatives,
     )
+    return pl.pallas_call(
+        deliver_kernel,
+        out_shape=(
+            jax.ShapeDtypeStruct((4, HV), F32),
+            jax.ShapeDtypeStruct((512, HV), BF16),
+        ),
+        in_specs=[VM, VM],
+        out_specs=(ANY, ANY),
+        scratch_shapes=[pltpu.SemaphoreType.DMA((2,))],
+        compiler_params=pltpu.CompilerParams(vmem_limit_bytes=8 * 2**20),
+        name="deliver",
+    )(item_grads, weight_grad)
 
 
 def solution(mesh):

time: 90.2 us -> 88.7 us (0.983)
  local copies, waits for them, and re-layouts: 1.94 us -> 0 us
    unnamed x2 -> x0, local copies, waits for them, and re-layouts: 1.94 us -> none
    pallas_call x0 -> x1, Pallas kernels: none -> 1.34 us  [local(): pl.pallas_call(deliver_kernel, out_shape=(jax.ShapeDtypeStruct((4, HV), F...]
    pallas_call x1, Pallas kernels: 87.6 us -> 86.6 us  [local(): pl.pallas_call(whole_kernel, out_shape=(vm(4, HV, dtype=F32), vm(512, HV)...]
where the time goes in v4:
time: 88.7 us; the launch traced here: 88.6 us
  Pallas kernels  87.9 us (99%)
    pallas_call x1, Pallas kernels, local(): pl.pallas_call(whole_kernel, out_shape=(vm(4, HV, dtype=F32), vm(512, HV)...  86.6 us

profile of v4, /device:TPU:1, one launch (start us, length us, event | category | flops | bytes accessed | tf_op | source)
XLA Modules:
  0.0 88.6 jit_solution(1323908759891799126)
XLA Ops:
  0.6 86.6 %whole.1 = (f32[4,2048]{1,0:T(4,128)S(1)}, bf16[512,2048]{1,0:T(8,128)(2,1)S(1)}) custom-call(s32[4]{0:T(128)} %lengths_h.1, bf16[4,256,1024]{2,1,0:T(8,128)(2,1)} %states_h.1, f32[4,16,256]{2,1,0:T(8,128)} %scores_h.1, f32[1,1024]{1,0:T(1,128)} %bitcast.3, bf16[1024,2048]{1,0:T(8,128)(2,1)} %vweight_h.1, bf16[256,2048]{1,0:T(8,128)(2,1)} %pos_h.1, ...), custom_call_target="tpu_custom_call" | custom-call | tf_op jit(solution)/shard_map/whole/pallas_call | solution.py:517
  87.2 1.3 %deliver.1 = (f32[4,2048]{1,0:T(4,128)}, bf16[512,2048]{1,0:T(8,128)(2,1)}) custom-call(f32[4,2048]{1,0:T(4,128)S(1)} %get-tuple-element.4.item_grads, bf16[512,2048]{1,0:T(8,128)(2,1)S(1)} %get-tuple-element.5.weight_grad), custom_call_target="tpu_custom_call" | custom-call | tf_op jit(solution)/shard_map/deliver/pallas_call | solution.py:557

commit v5 on v4

--- a/solution.py
+++ b/solution.py
@@ -359,7 +359,7 @@
     moved = grad_t * logits
     cat_along = jnp.sum(moved, axis=1, keepdims=True) * cat_inv
     along = jnp.sum(moved.T, axis=1, keepdims=True) * out_inv
-    by_row, by_row_lo = split((grad_t * (20.0 * cat_inv)).T)
+    by_row = (grad_t * (20.0 * cat_inv)).T.astype(BF16)
     inner = jnp.zeros((256, 1), F32)
     s1_copies, q1_copies, r1_copies, s2_copies, q2_copies = [], [], [], [], []
 
@@ -376,7 +376,7 @@
             s2_copies.append(net.put(s1.at[k - 1:k + 1, rows], s2_in.at[o - 1, k - 1:k + 1], peer(dy=o)))
 
     for k, j in enumerate(js):
-        g = mm(by_row, ce[0, k]) + mm(by_row_lo, ce[0, k])
+        g = mm(by_row, ce[0, k])
         g = (g - u_v[:, j] * along) * out_inv
         ug_v[:, j] = g
         rows = (inv * g).astype(BF16)

time: 88.7 us -> 88.3 us (level)
  no operation moved by 1% of the time
where the time goes in v5:
time: 88.3 us; the launch traced here: 88.2 us
  Pallas kernels  87.5 us (99%)
    pallas_call x1, Pallas kernels, local(): pl.pallas_call(whole_kernel, out_shape=(vm(4, HV, dtype=F32), vm(512, HV)...  86.2 us

profile of v5, /device:TPU:1, one launch (start us, length us, event | category | flops | bytes accessed | tf_op | source)
XLA Modules:
  0.0 88.2 jit_solution(10284619489504795264)
XLA Ops:
  0.6 86.2 %whole.1 = (f32[4,2048]{1,0:T(4,128)S(1)}, bf16[512,2048]{1,0:T(8,128)(2,1)S(1)}) custom-call(s32[4]{0:T(128)} %lengths_h.1, bf16[4,256,1024]{2,1,0:T(8,128)(2,1)} %states_h.1, f32[4,16,256]{2,1,0:T(8,128)} %scores_h.1, f32[1,1024]{1,0:T(1,128)} %bitcast.3, bf16[1024,2048]{1,0:T(8,128)(2,1)} %vweight_h.1, bf16[256,2048]{1,0:T(8,128)(2,1)} %pos_h.1, ...), custom_call_target="tpu_custom_call" | custom-call | tf_op jit(solution)/shard_map/whole/pallas_call | solution.py:517
  86.8 1.3 %deliver.1 = (f32[4,2048]{1,0:T(4,128)}, bf16[512,2048]{1,0:T(8,128)(2,1)}) custom-call(f32[4,2048]{1,0:T(4,128)S(1)} %get-tuple-element.4.item_grads, bf16[512,2048]{1,0:T(8,128)(2,1)S(1)} %get-tuple-element.5.weight_grad), custom_call_target="tpu_custom_call" | custom-call | tf_op jit(solution)/shard_map/deliver/pallas_call | solution.py:557
